TPU v7x, 32 devices: a whole 2x2x4 slice. The times are simulated.
32 devices in a mesh: freq: 8 (over z, x), rcv: 4 (over y, core).
Axes of the slice: x: 2, y: 2, z: 4, core: 2. Of those that a mesh axis runs over, the one named last changes fastest.
Arguments:
- primaries_start: float32 [512, 1024, 128], P(('rcv', 'freq')), may hold values from -6 to 6
- surface_operator: bfloat16 [512, 2, 384, 512], P('freq', None, 'rcv'), may hold values from -0.25 to 0.25
- data_spectra: bfloat16 [384, 512, 2, 128], P('rcv', 'freq'), may hold values from -6 to 6
- shrinkage: float32 [128], replicated, may hold values from 0.2 to 2
Outputs:
- primaries: float32 [512, 1024, 128], P(('rcv', 'freq'))
- residual_spectra: bfloat16 [384, 512, 2, 128], P('rcv', 'freq')
All inputs are finite; a program needn't handle non-finite values.
Results may differ from a plain program's by a relative error of at most 0.0085.
Values may be sent and summed in bfloat16 or wider, within the bound.
A program may use at most 192 MiB of HBM per device.

v0:
```python
import math

import jax
import jax.numpy as jnp
from jax import lax
from jax.sharding import PartitionSpec as P

S = 128
NS = 512
T_SIZE = 1024
ITERS = 2
NF = 512


def transform_table(frequencies, samples):
    freq_index = jnp.arange(frequencies, dtype=jnp.int32)[:, None]
    sample_index = jnp.arange(samples, dtype=jnp.int32)[None, :]
    phase = freq_index * sample_index % samples
    angle = phase.astype(jnp.float32) * (2.0 * math.pi / samples)
    factor = math.sqrt(2.0 / samples)
    return jnp.stack([factor * jnp.cos(angle), -factor * jnp.sin(angle)], axis=1).astype(
        jnp.bfloat16
    )


def forward_product(block, piece):
    real_op = block[:, 0]
    imag_op = block[:, 1]
    real_in = piece[:, :, 0]
    imag_in = piece[:, :, 1]

    def product(left, right):
        return jnp.einsum("krn,nks->rks", left, right, preferred_element_type=jnp.float32)

    real_out = product(real_op, real_in) - product(imag_op, imag_in)
    imag_out = product(real_op, imag_in) + product(imag_op, real_in)
    return jnp.stack([real_out, imag_out], axis=2)


def adjoint_product(block, resid):
    real_op = block[:, 0]
    imag_op = block[:, 1]
    real_res = resid[:, :, 0]
    imag_res = resid[:, :, 1]

    def product(left, right):
        return jnp.einsum("krn,rks->nks", left, right, preferred_element_type=jnp.float32)

    real_dir = product(real_op, real_res) + product(imag_op, imag_res)
    imag_dir = product(real_op, imag_res) - product(imag_op, real_res)
    return jnp.stack([real_dir, imag_dir], axis=2)


def local(primaries_start, surface_operator, data_spectra, shrinkage):
    table = transform_table(NF, T_SIZE)
    primaries = primaries_start
    count_total = 2.0 * NF * NS * S
    residual = data_spectra
    operator_full = lax.all_gather(surface_operator, "rcv", axis=2, tiled=True)
    source_data = lax.all_to_all(data_spectra, "rcv", split_axis=3, concat_axis=0, tiled=True)
    for iteration in range(ITERS):
        local_spectra = jnp.einsum(
            "kct,nts->nkcs",
            table,
            primaries.astype(jnp.bfloat16),
            preferred_element_type=jnp.float32,
        ).astype(jnp.bfloat16)
        spectra = lax.all_to_all(local_spectra, "freq", split_axis=1, concat_axis=0, tiled=True)
        source_spectra = lax.all_to_all(spectra, "rcv", split_axis=3, concat_axis=0, tiled=True)
        predicted = forward_product(operator_full, source_spectra)
        residual = (source_data.astype(jnp.float32) - predicted).astype(jnp.bfloat16)
        residual_sq = jnp.sum(jnp.square(residual.astype(jnp.float32)))
        direction = adjoint_product(operator_full, residual)
        direction_sq = jnp.sum(jnp.square(direction))
        residual_norm, direction_norm = lax.psum((residual_sq, direction_sq), ("freq", "rcv"))
        step_size = 0.5 * residual_norm / (direction_norm + 1e-06)
        threshold = shrinkage[None, None, :] * (step_size * jnp.sqrt(direction_norm / count_total))
        direction_low = direction.astype(jnp.bfloat16)
        direction_low = lax.all_to_all(
            direction_low, "rcv", split_axis=0, concat_axis=3, tiled=True
        )
        update = jnp.einsum(
            "kct,nkcs->nts",
            table,
            lax.all_to_all(direction_low, "freq", split_axis=0, concat_axis=1, tiled=True),
            preferred_element_type=jnp.float32,
        )
        moved = primaries + step_size * update
        primaries = moved - jnp.clip(moved, -threshold, threshold)
    residual = lax.all_to_all(residual, "rcv", split_axis=0, concat_axis=3, tiled=True)
    return (primaries, residual)


def solution(mesh):
    return jax.shard_map(
        local,
        mesh=mesh,
        in_specs=(
            P(("rcv", "freq"), None, None),
            P("freq", None, "rcv", None),
            P("rcv", "freq", None, None),
            P(),
        ),
        out_specs=(P(("rcv", "freq"), None, None), P("rcv", "freq", None, None)),
        check_vma=False,
    )
```

profile of v0, /device:TPU:0, one launch (start us, length us, event | category | flops | bytes accessed | tf_op | source)
XLA Modules:
  0.0 1400.8 jit_solution(242871086299409631)
XLA Ops:
  7.2 10.7 copy.117
  18.0 8.6 multiply_convert_fusion
  26.5 11.3 convert_bitcast_fusion.2
  42.7 7.7 all-to-all-start.1
  50.4 10.5 copy.109
  60.9 82.7 %all-to-all-done.1 = bf16[16,512,2,128]{3,0,2,1:T(8,128)(2,1)} async-done(((bf16[16,512,2,128]{3,0,2,1:T(8,128)(2,1)}), bf16[16,512,2,128]{3,0,2,1:T(8,128)(2,1)}, u32[]{:S(2)}, u32[]{:S(2)}) %all-to-all-start.1) | async-done | bytes 4194336 | tf_op jit(solution)/shard_map/all_to_all | solution.py:68
  148.4 6.1 copy.113
  154.6 7.4 copy.114
  161.9 80.0 %all-to-all-done = bf16[96,64,2,128]{0,2,1,3:T(2,128)(2,1)} async-done(((bf16[96,64,2,128]{0,2,1,3:T(2,128)(2,1)}), bf16[96,64,2,128]{0,2,1,3:T(2,128)(2,1)}, u32[]{:S(2)}, u32[]{:S(2)}) %all-to-all-start) | async-done | bytes 3145760 | tf_op jit(solution)/shard_map/all_to_all | solution.py:60
  247.0 12.0 convert_bitcast_fusion
  259.0 15.3 %copy.120 = f32[4,96,64,2,32]{1,0,4,2,3:T(4,128)} copy(f32[4,96,64,2,32]{1,4,0,3,2:T(8,128)} %get-tuple-element.20) | data formatting | bytes 12582912 | tf_op jit(solution)/shard_map/convert_element_type | solution.py:71
  274.4 9.8 reshape.98
  284.1 56.1 %all-to-all-done.2 = bf16[128,64,2,128]{0,1,2,3:T(8,128)(2,1)} async-done(((bf16[128,64,2,128]{0,1,2,3:T(8,128)(2,1)}), bf16[128,64,2,128]{0,1,2,3:T(8,128)(2,1)}, u32[]{:S(2)}, u32[]{:S(2)}) %all-to-all-start.2) | async-done | bytes 4194336 | tf_op jit(solution)/shard_map/all_to_all | solution.py:69
  340.3 7.7 copy.116
  348.0 7.2 all_to_all.132
  355.2 55.2 %all-gather.2.cloned.1.call-done = bf16[64,2,384,512]{3,2,0,1:T(8,128)(2,1)} async-done(((bf16[64,2,96,512]{3,2,0,1:T(8,128)(2,1)}), bf16[64,2,384,512]{3,2,0,1:T(8,128)(2,1)}) %all-gather.2.cloned.1.call-update) | async-done | bytes 50331664 | tf_op jit(solution)/shard_map/all_gather | solution.py:59
  410.4 14.2 %fusion.13 = f32[64,32,384]{2,1,0:T(8,128)} fusion(bf16[64,2,384,512]{3,2,0,1:T(8,128)(2,1)} %all-gather.2.cloned.1.call-done, bf16[512,64,2,32]{0,3,1,2:T(8,128)(2,1)} %all_to_all.132), kind=kOutput, calls=%fused_computation.32 | convolution fusion | flops 805306368 | bytes 30408704 | tf_op jit(solution)/shard_map/krn,nks->rks/dot_general | solution.py:33
  424.5 13.2 fusion.12
  437.7 15.6 %fusion.42 = f32[64,32,384]{2,1,0:T(8,128)} fusion(f32[64,32,384]{2,1,0:T(8,128)} %fusion.13, bf16[64,2,384,512]{3,2,0,1:T(8,128)(2,1)} %all-gather.2.cloned.1.call-done, bf16[512,64,2,32]{0,3,1,2:T(8,128)(2,1)} %all_to_all.132), kind=kOutput, calls=%fused_computation.77 | convolution fusion | flops 806092800 | bytes 33554432 | tf_op jit(solution)/shard_map/krn,nks->rks/dot_general | solution.py:33
  453.3 14.5 %fusion.43 = f32[64,32,384]{2,1,0:T(8,128)} fusion(f32[64,32,384]{2,1,0:T(8,128)S(1)} %fusion.12, bf16[64,2,384,512]{3,2,0,1:T(8,128)(2,1)} %all-gather.2.cloned.1.call-done, bf16[512,64,2,32]{0,3,1,2:T(8,128)(2,1)} %all_to_all.132), kind=kOutput, calls=%fused_computation.78 | convolution fusion | flops 806092800 | bytes 33554432 | tf_op jit(solution)/shard_map/krn,nks->rks/dot_general | solution.py:33
  467.8 5.9 fusion.4
  473.7 12.6 fusion.11
  486.3 12.4 fusion.10
  498.7 13.8 add_bitcast_fusion.1
  512.5 14.1 %subtract_bitcast_fusion.1 = f32[512,64,1,32]{0,3,1,2:T(8,128)} fusion(f32[64,32,512]{2,1,0:T(8,128)} %fusion.10, bf16[64,2,384,512]{3,2,0,1:T(8,128)(2,1)} %all-gather.2.cloned.1.call-done, bf16[384,64,2,32]{0,3,1,2:T(8,128)(2,1)S(1)} %fusion.4), kind=kOutput, calls=%fused_computation.49 | convolution fusion | flops 806354944 | bytes 35127296 | tf_op jit(solution)/shard_map/krn,rks->nks/dot_general | solution.py:47
  526.6 6.2 fusion.3
  532.8 15.5 %copy.121 = bf16[512,64,2,32]{1,3,2,0:T(8,128)(2,1)} copy(bf16[512,64,2,32]{0,3,1,2:T(8,128)(2,1)} %fusion.3) | data formatting | bytes 8388608 | tf_op jit(solution)/shard_map/convert_element_type | solution.py:78
  548.3 9.6 reshape.106
  557.9 53.9 %all_to_all.171 = bf16[4,2,262144]{2,1,0:T(2,128)(2,1)} all-to-all(bf16[4,2,262144]{2,1,0:T(2,128)(2,1)} %reshape.106), channel_id=1, replica_groups=mesh['freq'=8,'rcv'=4] {'rcv'}, dimensions={0} | all-to-all | bytes 8388608 | tf_op jit(solution)/shard_map/all_to_all | solution.py:79
  611.7 9.3 reshape.107
  621.0 12.0 copy.156
  638.5 11.3 copy.124
  678.5 9.3 copy.128
  687.8 80.6 %all-reduce.1 = (f32[]{:T(128)}, f32[]{:T(128)}) all-reduce(f32[]{:T(128)} %multiply_reduce_fusion.3, f32[]{:T(128)} %multiply_reduce_fusion.2), channel_id=1, replica_groups=mesh['freq'=8,'rcv'=4] {'freq','rcv'}, use_global_device_ids=true, to_apply=%region_1.2 | all-reduce | flops 2 | bytes 16 | tf_op jit(solution)/shard_map/psum | solution.py:75
  785.8 6.2 convert_bitcast_fusion.1
  792.0 11.3 copy.129
  803.3 97.3 %all_to_all.172 = bf16[16,512,2,128]{3,2,0,1:T(2,128)(2,1)S(1)} all-to-all(bf16[16,512,2,128]{3,2,0,1:T(2,128)(2,1)} %copy.129), channel_id=1, replica_groups=mesh['freq'=8,'rcv'=4] {'freq'}, dimensions={1} | all-to-all | bytes 8388608 | tf_op jit(solution)/shard_map/all_to_all | solution.py:68
  905.2 7.5 copy.132
  912.7 52.3 %all_to_all.173 = bf16[128,64,2,128]{0,1,2,3:T(8,128)(2,1)S(1)} all-to-all(bf16[128,64,2,128]{0,1,2,3:T(8,128)(2,1)} %copy.132), channel_id=1, replica_groups=mesh['freq'=8,'rcv'=4] {'rcv'}, dimensions={3} | all-to-all | bytes 8388608 | tf_op jit(solution)/shard_map/all_to_all | solution.py:69
  970.3 7.2 all_to_all.148
  977.4 14.2 %fusion.9 = f32[64,32,384]{2,1,0:T(8,128)} fusion(bf16[64,2,384,512]{3,2,0,1:T(8,128)(2,1)} %all-gather.2.cloned.1.call-done, bf16[512,64,2,32]{0,3,1,2:T(8,128)(2,1)} %all_to_all.148), kind=kOutput, calls=%fused_computation.28 | convolution fusion | flops 805306368 | bytes 30408704 | tf_op jit(solution)/shard_map/krn,nks->rks/dot_general | solution.py:33
  991.6 13.2 fusion.8
  1004.8 15.3 %fusion.44 = f32[64,32,384]{2,1,0:T(8,128)} fusion(f32[64,32,384]{2,1,0:T(8,128)} %fusion.9, bf16[64,2,384,512]{3,2,0,1:T(8,128)(2,1)} %all-gather.2.cloned.1.call-done, bf16[512,64,2,32]{0,3,1,2:T(8,128)(2,1)} %all_to_all.148), kind=kOutput, calls=%fused_computation.79 | convolution fusion | flops 806092800 | bytes 33554432 | tf_op jit(solution)/shard_map/krn,nks->rks/dot_general | solution.py:33
  1020.1 14.6 %fusion.45 = f32[64,32,384]{2,1,0:T(8,128)} fusion(f32[64,32,384]{2,1,0:T(8,128)S(1)} %fusion.8, bf16[64,2,384,512]{3,2,0,1:T(8,128)(2,1)} %all-gather.2.cloned.1.call-done, bf16[512,64,2,32]{0,3,1,2:T(8,128)(2,1)} %all_to_all.148), kind=kOutput, calls=%fused_computation.80 | convolution fusion | flops 806092800 | bytes 33554432 | tf_op jit(solution)/shard_map/krn,nks->rks/dot_general | solution.py:33
  1034.7 5.9 fusion.5
  1040.6 12.5 fusion.7
  1053.1 12.5 fusion.6
  1065.5 13.6 add_bitcast_fusion
  1079.2 13.6 subtract_bitcast_fusion
  1092.8 6.2 fusion.2
  1099.0 15.6 %copy.137 = bf16[512,64,2,32]{1,3,2,0:T(8,128)(2,1)} copy(bf16[512,64,2,32]{0,3,1,2:T(8,128)(2,1)} %fusion.2) | data formatting | bytes 8388608 | tf_op jit(solution)/shard_map/convert_element_type | solution.py:78
  1114.6 9.5 reshape.108
  1129.2 11.7 copy.144
  1140.9 7.8 reshape.110
  1148.7 28.8 %all-to-all-done.7 = bf16[4,2,262144]{2,1,0:T(2,128)(2,1)} async-done(((bf16[4,2,262144]{2,1,0:T(2,128)(2,1)}), bf16[4,2,262144]{2,1,0:T(2,128)(2,1)}, u32[]{:S(2)}, u32[]{:S(2)}) %all-to-all-start.7) | async-done | bytes 4194336 | tf_op jit(solution)/shard_map/all_to_all | solution.py:79
  1182.1 9.3 reshape.109
  1191.4 12.0 copy.158
  1208.9 11.3 copy.140
  1248.2 91.3 %all-reduce = (f32[]{:T(128)}, f32[]{:T(128)}) all-reduce(f32[]{:T(128)} %multiply_reduce_fusion.1, f32[]{:T(128)} %multiply_reduce_fusion), channel_id=1, replica_groups=mesh['freq'=8,'rcv'=4] {'freq','rcv'}, use_global_device_ids=true, to_apply=%region_5.6 | all-reduce | flops 2 | bytes 16 | tf_op jit(solution)/shard_map/psum | solution.py:75
  1341.4 7.6 reshape.111
  1348.9 12.6 copy.145
  1361.6 8.5 copy.147
  1376.5 7.8 minimum_subtract_fusion
  1384.3 9.2 copy.146
  (90 shorter events, 123.6 us)
Async XLA Ops:
  7.2 403.2 %all-gather.2.cloned.1.call-start = ((), (), s32[]{:S(2)}) async-start(), calls=%async_computation.10 | async-start | bytes 62914560 | tf_op jit(solution)/shard_map/all_gather | solution.py:59
  26.5 11.3 copy-start.13
  26.5 11.3 copy-start.16
  42.7 7.7 copy-start.19
  42.7 100.9 %all-to-all-start.1 = ((bf16[16,512,2,128]{3,0,2,1:T(8,128)(2,1)}), bf16[16,512,2,128]{3,0,2,1:T(8,128)(2,1)}, u32[]{:S(2)}, u32[]{:S(2)}) async-start(bf16[16,512,2,128]{3,0,2,1:T(8,128)(2,1)} %copy.111), calls=%async_computation.1 | async-start | bytes 8388608 | tf_op jit(solution)/shard_map/all_to_all | solution.py:68
  143.6 98.4 %all-to-all-start = ((bf16[96,64,2,128]{0,2,1,3:T(2,128)(2,1)}), bf16[96,64,2,128]{0,2,1,3:T(2,128)(2,1)}, u32[]{:S(2)}, u32[]{:S(2)}) async-start(bf16[96,64,2,128]{0,2,1,3:T(2,128)(2,1)} %copy.109), calls=%async_computation | async-start | bytes 8388608 | tf_op jit(solution)/shard_map/all_to_all | solution.py:60
  241.9 98.3 %all-to-all-start.2 = ((bf16[128,64,2,128]{0,1,2,3:T(8,128)(2,1)}), bf16[128,64,2,128]{0,1,2,3:T(8,128)(2,1)}, u32[]{:S(2)}, u32[]{:S(2)}) async-start(bf16[128,64,2,128]{0,1,2,3:T(8,128)(2,1)} %copy.114), calls=%async_computation.2 | async-start | bytes 8388608 | tf_op jit(solution)/shard_map/all_to_all | solution.py:69
  649.8 5.7 copy-start.4
  649.8 120.8 %all-to-all-start.4 = ((bf16[128,64,2,128]{3,2,1,0:T(2,128)(2,1)}), bf16[128,64,2,128]{3,2,1,0:T(2,128)(2,1)}, u32[]{:S(2)}, u32[]{:S(2)}) async-start(bf16[128,64,2,128]{3,2,1,0:T(2,128)(2,1)} %copy.124), calls=%async_computation.4 | async-start | bytes 8388608 | tf_op jit(solution)/shard_map/all_to_all | solution.py:85
  659.1 4.9 copy-start.3
  667.5 3.4 copy-start.9
  667.5 4.7 copy-start.10
  672.3 2.8 copy-start.5
  672.3 3.5 copy-start.11
  678.5 92.0 %copy-start.20 = (f32[128]{0:T(128)S(1)}, f32[128]{0:T(128)}, u32[]{:S(2)}) copy-start(f32[128]{0:T(128)} %param.7) | copy-start | bytes 1540
  770.6 5.1 slice-start.2
  774.2 2.2 slice-start.3
  774.2 2.5 copy-start.14
  774.2 2.8 copy-start.17
  782.4 3.4 copy-start
  1124.1 53.3 %all-to-all-start.7 = ((bf16[4,2,262144]{2,1,0:T(2,128)(2,1)}), bf16[4,2,262144]{2,1,0:T(2,128)(2,1)}, u32[]{:S(2)}, u32[]{:S(2)}) async-start(bf16[4,2,262144]{2,1,0:T(2,128)(2,1)} %reshape.108), calls=%async_computation.7 | async-start | bytes 8388608 | tf_op jit(solution)/shard_map/all_to_all | solution.py:79
  1177.5 42.8 %all-to-all-start.9 = ((bf16[4,2,196608]{2,1,0:T(2,128)(2,1)}), bf16[4,2,196608]{2,1,0:T(2,128)(2,1)}, u32[]{:S(2)}, u32[]{:S(2)}) async-start(bf16[4,2,196608]{2,1,0:T(2,128)(2,1)} %reshape.110), calls=%async_computation.9 | async-start | bytes 6291456 | tf_op jit(solution)/shard_map/all_to_all | solution.py:90
  1220.2 4.8 copy-start.2
  1220.2 149.8 %all-to-all-start.8 = ((bf16[128,64,2,128]{3,2,1,0:T(2,128)(2,1)}), bf16[128,64,2,128]{3,2,1,0:T(2,128)(2,1)}, u32[]{:S(2)}, u32[]{:S(2)}) async-start(bf16[128,64,2,128]{3,2,1,0:T(2,128)(2,1)} %copy.140), calls=%async_computation.8 | async-start | bytes 8388608 | tf_op jit(solution)/shard_map/all_to_all | solution.py:85
  1228.8 4.8 copy-start.1
  1237.3 3.4 copy-start.6
  1237.3 4.7 copy-start.12
  1242.0 2.8 copy-start.7
  1242.0 3.5 copy-start.8
  1245.5 95.9 %copy-start.21 = (f32[128]{0:T(128)S(1)}, f32[128]{0:T(128)}, u32[]{:S(2)}) copy-start(f32[128]{0:T(128)} %param.7) | copy-start | bytes 1540
  1370.0 5.1 slice-start
  1373.7 2.2 slice-start.1
  1373.7 2.5 copy-start.15
  1373.7 2.8 copy-start.18
Sparse Core Ops, SparseCore 0:
  18.1 392.2 all-gather.1
where the time goes:
time: 1410 us; the launch traced here: 1400 us
  blocking collectives  375 us (27%)
  local copies, waits for them, and re-layouts  360 us (26%)
  waiting for transfers between devices  303 us (21%)
  matrix products  250 us (18%)
  other arithmetic  55.9 us (4%)
  starting transfers between devices  37.9 us (3%)
  between operations  18.8 us (1%)
    psum x2, blocking collectives, local(): lax.psum((residual_sq, direction_sq), ('freq', 'rcv'))  172 us
    dot_general x8, matrix products, product(): jnp.einsum('krn,nks->rks', left, right, preferred_element_type=jnp.float32)  115 us
    unnamed x63, local copies, waits for them, and re-layouts  112 us
    dot_general x8, matrix products, product(): jnp.einsum('krn,rks->nks', left, right, preferred_element_type=jnp.float32)  105 us
    all_to_all x1, blocking collectives, local(): lax.all_to_all(local_spectra, 'freq', split_axis=1, concat_axis=0, tiled=...  97.3 us
    all_to_all x1, waiting for transfers between devices, local(): lax.all_to_all(local_spectra, 'freq', split_axis=1, concat_axis=0, tiled=...  82.7 us
    all_to_all x1, waiting for transfers between devices, local(): lax.all_to_all(data_spectra, 'rcv', split_axis=3, concat_axis=0, tiled=True)  80 us
    all_to_all x6, local copies, waits for them, and re-layouts, local(): lax.all_to_all(direction_low, 'rcv', split_axis=0, concat_axis=3, tiled=T...  57.6 us
  transfers between devices with their start and end apart: 8, of which 5 were waited for; matrix products, arithmetic and copies ran while one was open for 16% of the time, Pallas kernels for 0%

commit v1 on v0

v1 whole, which is shorter than its diff:
```python
import functools
import math

import jax
import jax.numpy as jnp
from jax import lax
from jax.experimental import pallas as pl
from jax.experimental.pallas import tpu as pltpu
from jax.sharding import PartitionSpec as P

ITERS = 2
CORES = 2
MESH = pl.DeviceIdType.MESH
VMEM_LIMIT = 48 * 1024 * 1024


def transform_table(frequencies, samples):
    freq_index = jnp.arange(frequencies, dtype=jnp.int32)[:, None]
    sample_index = jnp.arange(samples, dtype=jnp.int32)[None, :]
    phase = freq_index * sample_index % samples
    angle = phase.astype(jnp.float32) * (2.0 * math.pi / samples)
    factor = math.sqrt(2.0 / samples)
    return jnp.stack([factor * jnp.cos(angle), -factor * jnp.sin(angle)], axis=1).astype(
        jnp.bfloat16
    )


def place(groups):
    freq = lax.axis_index("freq")
    rcv = lax.axis_index("rcv")
    return freq, rcv // CORES, lax.rem(rcv, CORES)


def peers_of(freqs, offset, freq, core):
    step, flip = offset // CORES, offset % CORES
    to_freq = lax.rem(freq + step, freqs)
    from_freq = lax.rem(freq + freqs - step, freqs)
    other = lax.rem(core + flip, CORES)
    return to_freq, from_freq, other


def enter(freqs, groups, freq, group, core):
    barrier = pltpu.get_barrier_semaphore()
    for offset in range(1, freqs * CORES):
        to_freq, _, other = peers_of(freqs, offset, freq, core)
        pl.semaphore_signal(
            barrier, inc=1, device_id=(to_freq, group * CORES + other), device_id_type=MESH
        )
    for hop in range(1, groups):
        there = lax.rem(group + hop, groups)
        pl.semaphore_signal(
            barrier, inc=1, device_id=(freq, there * CORES + core), device_id_type=MESH
        )
    pl.semaphore_wait(barrier, freqs * CORES - 1 + groups - 1)


def spread_kernel(freqs, groups, with_operator, *refs):
    if with_operator:
        spec, oper, data, gathered, oper_out, data_out, *sems = refs
        send, recv, send_y, recv_y, local, swap_send, swap_recv = sems
    else:
        spec, gathered, send, recv, send_y, recv_y, local = refs
    freq, group, core = place(groups)
    count = freqs * CORES
    enter(freqs, groups, freq, group, core)

    def slot(source_freq, source_core, source_group=group):
        return (source_group * CORES + source_core) * freqs + source_freq

    def direct(offset):
        to_freq, _, other = peers_of(freqs, offset, freq, core)
        return pltpu.make_async_remote_copy(
            src_ref=spec.at[to_freq * CORES + other],
            dst_ref=gathered.at[slot(freq, core)],
            send_sem=send.at[offset],
            recv_sem=recv.at[offset],
            device_id=(to_freq, group * CORES + other),
            device_id_type=MESH,
        )

    def forward(offset, hop):
        _, from_freq, other = peers_of(freqs, offset, freq, core)
        there = lax.rem(group + hop, groups)
        place_of = slot(from_freq, other)
        source = spec.at[freq * CORES + core] if offset == 0 else gathered.at[place_of]
        return pltpu.make_async_remote_copy(
            src_ref=source,
            dst_ref=gathered.at[place_of],
            send_sem=send_y.at[(hop - 1) * count + offset],
            recv_sem=recv_y.at[(hop - 1) * count + offset],
            device_id=(freq, there * CORES + core),
            device_id_type=MESH,
        )

    order = list(range(1, count))
    for offset in order:
        direct(offset).start()
    own = pltpu.make_async_copy(
        spec.at[freq * CORES + core], gathered.at[slot(freq, core)], local.at[0]
    )
    own.start()
    for hop in range(1, groups):
        forward(0, hop).start()
    others = []
    if with_operator:
        sibling = 1 - core
        held = oper.shape[2]
        rows = pl.ds(pl.multiple_of(core * held, 16), held)
        kept = oper_out.shape[0]
        for number, (source, target, first) in enumerate(
            [
                (
                    oper.at[pl.ds(sibling * kept, kept)],
                    oper_out.at[:, :, rows, :],
                    oper.at[pl.ds(core * kept, kept)],
                ),
                (data.at[sibling], data_out.at[:, rows, :], data.at[core]),
            ]
        ):
            away = pltpu.make_async_remote_copy(
                src_ref=source,
                dst_ref=target,
                send_sem=swap_send.at[number],
                recv_sem=swap_recv.at[number],
                device_id=(freq, group * CORES + sibling),
                device_id_type=MESH,
            )
            away.start()
            here = pltpu.make_async_copy(first, target, local.at[1 + number])
            here.start()
            others += [away, here]
    for offset in order:
        direct(offset).wait_recv()
        for hop in range(1, groups):
            forward(offset, hop).start()
    own.wait()
    for offset in order:
        direct(offset).wait_send()
    for hop in range(1, groups):
        for offset in range(count):
            forward(offset, hop).wait()
    for copy in others:
        copy.wait()


def collect_kernel(freqs, groups, with_residual, *refs):
    if with_residual:
        part, resid, total, square, resid_out, landed, ready, mine, *sems = refs
        send, recv, send_y, recv_y, local, swap_send, swap_recv = sems
    else:
        part, total, square, landed, ready, mine, send, recv, send_y, recv_y, local = refs
    freq, group, core = place(groups)
    count = freqs * CORES
    rows = part.shape[1]
    enter(freqs, groups, freq, group, core)

    def slot(freq_of, core_of, group_of):
        return (group_of * CORES + core_of) * freqs + freq_of

    def across(offset, hop):
        to_freq, _, other = peers_of(freqs, offset, freq, core)
        there = lax.rem(group + hop, groups)
        number = (hop - 1) * count + offset
        return pltpu.make_async_remote_copy(
            src_ref=part.at[slot(to_freq, other, there)],
            dst_ref=landed.at[number],
            send_sem=send_y.at[number],
            recv_sem=recv_y.at[number],
            device_id=(freq, there * CORES + core),
            device_id_type=MESH,
        )

    def fetch(offset):
        to_freq, _, other = peers_of(freqs, offset, freq, core)
        return pltpu.make_async_copy(
            part.at[slot(to_freq, other, group)], mine.at[offset], local.at[offset]
        )

    def direct(offset):
        to_freq, _, other = peers_of(freqs, offset, freq, core)
        return pltpu.make_async_remote_copy(
            src_ref=ready.at[offset],
            dst_ref=total.at[freq * CORES + core],
            send_sem=send.at[offset],
            recv_sem=recv.at[offset],
            device_id=(to_freq, group * CORES + other),
            device_id_type=MESH,
        )

    order = list(range(count - 1, -1, -1))
    others = []
    for offset in order:
        for hop in range(1, groups):
            across(offset, hop).start()
        fetch(offset).start()
    if with_residual:
        sibling = 1 - core
        held = resid.shape[2]
        kept = resid.shape[1]
        rows_of = resid_out.shape[0] // CORES
        away = pltpu.make_async_remote_copy(
            src_ref=resid.at[sibling],
            dst_ref=resid_out.at[pl.ds(core * kept, kept)],
            send_sem=swap_send.at[0],
            recv_sem=swap_recv.at[0],
            device_id=(freq, group * CORES + sibling),
            device_id_type=MESH,
        )
        away.start()
        here = pltpu.make_async_copy(
            resid.at[core], resid_out.at[pl.ds(core * kept, kept)], local.at[count]
        )
        here.start()
        others = [away, here]
    square[...] = jnp.zeros_like(square)
    tile = min(rows, 128)
    for offset in order:
        fetch(offset).wait()
        for hop in range(1, groups):
            across(offset, hop).wait_recv()

        @pl.loop(0, rows // tile)
        def add(step):
            here = pl.ds(pl.multiple_of(step * tile, tile), tile)
            value = mine[offset, here, :].astype(jnp.float32)
            for hop in range(1, groups):
                value += landed[(hop - 1) * count + offset, here, :].astype(jnp.float32)
            ready[offset, here, :] = value.astype(jnp.bfloat16)
            square[...] += jnp.sum((value * value).reshape(tile // 8, 8, -1), axis=0)

        if offset:
            direct(offset).start()
    last = pltpu.make_async_copy(ready.at[0], total.at[freq * CORES + core], local.at[count + 1])
    last.start()
    last.wait()
    for offset in range(1, count):
        direct(offset).wait()
    for hop in range(1, groups):
        for offset in range(count):
            across(offset, hop).wait_send()
    for copy in others:
        copy.wait()


def spread(freqs, groups, ident, spectra, operator=None, data=None):
    count = freqs * CORES
    _, rows, width = spectra.shape
    shapes = [jax.ShapeDtypeStruct((groups * count, rows, width), jnp.bfloat16)]
    dma = pltpu.SemaphoreType.DMA
    sems = [dma((count,)), dma((count,)), dma(((groups - 1) * count,)), dma(((groups - 1) * count,)), dma((3,))]
    args = [spectra]
    if operator is not None:
        kb, two, held, points = operator.shape
        _, kept, _, width = data.shape
        shapes += [
            jax.ShapeDtypeStruct((kb // CORES, two, held * CORES, points), jnp.bfloat16),
            jax.ShapeDtypeStruct((kept, held * CORES, width), jnp.bfloat16),
        ]
        sems += [dma((2,)), dma((2,))]
        args += [operator, data]
    anywhere = pl.BlockSpec(memory_space=pl.ANY)
    return pl.pallas_call(
        functools.partial(spread_kernel, freqs, groups, operator is not None),
        out_shape=shapes,
        in_specs=[anywhere] * len(args),
        out_specs=[anywhere] * len(shapes),
        scratch_shapes=sems,
        compiler_params=pltpu.CompilerParams(
            collective_id=ident, has_side_effects=True, vmem_limit_bytes=VMEM_LIMIT
        ),
    )(*args)


def collect(freqs, groups, ident, part, resid=None):
    count = freqs * CORES
    _, rows, width = part.shape
    dma = pltpu.SemaphoreType.DMA
    shapes = [
        jax.ShapeDtypeStruct((count, rows, width), jnp.bfloat16),
        jax.ShapeDtypeStruct((8, width), jnp.float32),
    ]
    scratch = [
        pltpu.VMEM(((groups - 1) * count, rows, width), jnp.bfloat16),
        pltpu.VMEM((count, rows, width), jnp.bfloat16),
        pltpu.VMEM((count, rows, width), jnp.bfloat16),
        dma((count,)), dma((count,)), dma(((groups - 1) * count,)), dma(((groups - 1) * count,)), dma((count + 2,)),
    ]
    anywhere = pl.BlockSpec(memory_space=pl.ANY)
    outs = [anywhere, pl.BlockSpec(memory_space=pltpu.VMEM)]
    args = [part]
    if resid is not None:
        _, kept, held, _ = resid.shape
        shapes.append(jax.ShapeDtypeStruct((kept * CORES, held, width), jnp.bfloat16))
        outs.append(anywhere)
        scratch += [dma((1,)), dma((1,))]
        args.append(resid)
    return pl.pallas_call(
        functools.partial(collect_kernel, freqs, groups, resid is not None),
        out_shape=shapes,
        in_specs=[anywhere] * len(args),
        out_specs=outs,
        scratch_shapes=scratch,
        compiler_params=pltpu.CompilerParams(
            collective_id=ident, has_side_effects=True, vmem_limit_bytes=VMEM_LIMIT
        ),
    )(*args)


def local(freqs, groups, primaries_start, surface_operator, data_spectra, shrinkage):
    points, samples, sources = primaries_start.shape
    band, _, held, all_points = surface_operator.shape
    kept = band // CORES
    count = freqs * CORES
    everywhere = groups * count
    frequencies = band * freqs
    width = 2 * sources
    table = transform_table(frequencies, samples)
    primaries = primaries_start
    count_total = 2.0 * frequencies * all_points * sources

    data = data_spectra.reshape(held, CORES, kept, width).transpose(1, 2, 0, 3)
    operator = recorded = None
    for iteration in range(ITERS):
        local_spectra = jnp.einsum(
            "kct,nts->kncs",
            table,
            primaries.astype(jnp.bfloat16),
            preferred_element_type=jnp.float32,
        ).astype(jnp.bfloat16).reshape(count, kept * points, width)
        if iteration == 0:
            spectra, operator, recorded = spread(
                freqs, groups, 0, local_spectra, surface_operator, data
            )
        else:
            (spectra,) = spread(freqs, groups, 2, local_spectra)
        spectra = spectra.reshape(everywhere, kept, points, width).transpose(1, 0, 2, 3)
        spectra = spectra.reshape(kept, all_points, width)
        resid, direction = products(operator, spectra, recorded)
        residual_sq = jnp.sum(jnp.square(resid.astype(jnp.float32)))
        part = direction.reshape(kept, everywhere, points, width).transpose(1, 0, 2, 3)
        part = part.reshape(everywhere, kept * points, width)
        if iteration < ITERS - 1:
            total, square = collect(freqs, groups, 1, part)
        else:
            halves = resid.reshape(kept, CORES, held, width).transpose(1, 0, 2, 3)
            total, square, residual = collect(freqs, groups, 3, part, halves)
        residual_norm, direction_norm = lax.psum(
            (residual_sq, jnp.sum(square)), ("freq", "rcv")
        )
        step_size = 0.5 * residual_norm / (direction_norm + 1e-06)
        threshold = shrinkage[None, None, :] * (step_size * jnp.sqrt(direction_norm / count_total))
        update = jnp.einsum(
            "kct,kncs->nts",
            table,
            total.reshape(frequencies, points, 2, sources),
            preferred_element_type=jnp.float32,
        )
        moved = primaries + step_size * update
        primaries = moved - jnp.clip(moved, -threshold, threshold)
    residual = residual.transpose(1, 0, 2).reshape(held, band, 2, sources)
    return (primaries, residual)


def products(operator, spectra, recorded):
    sources = spectra.shape[2] // 2
    real_op, imag_op = operator[:, 0], operator[:, 1]

    def turned(values, sign):
        return jnp.concatenate(
            [-sign * values[:, :, sources:], sign * values[:, :, :sources]], axis=2
        )

    def product(left, right, order):
        return jnp.einsum(order, left, right, preferred_element_type=jnp.float32)

    ahead = "krn,kns->krs"
    back = "krn,krs->kns"
    predicted = product(real_op, spectra, ahead) + product(imag_op, turned(spectra, 1), ahead)
    resid = (recorded.astype(jnp.float32) - predicted).astype(jnp.bfloat16)
    direction = product(real_op, resid, back) + product(imag_op, turned(resid, -1), back)
    return resid, direction.astype(jnp.bfloat16)


def solution(mesh):
    freqs = mesh.shape["freq"]
    groups = mesh.shape["rcv"] // CORES
    return jax.shard_map(
        functools.partial(local, freqs, groups),
        mesh=mesh,
        in_specs=(
            P(("rcv", "freq"), None, None),
            P("freq", None, "rcv", None),
            P("rcv", "freq", None, None),
            P(),
        ),
        out_specs=(P(("rcv", "freq"), None, None), P("rcv", "freq", None, None)),
        check_vma=False,
    )
```

time: 1410 us -> 937 us (0.66)
  Pallas kernels: 0 us -> 573 us
  waiting for transfers between devices: 303 us -> 0 us
  blocking collectives: 375 us -> 77.6 us
  local copies, waits for them, and re-layouts: 360 us -> 124 us
  matrix products: 250 us -> 127 us
  starting transfers between devices: 37.9 us -> 0 us
  other arithmetic: 55.9 us -> 20.7 us
    pallas_call x0 -> x4, Pallas kernels: none -> 573 us  [the longest x2 323 us: spread(): pl.pallas_call(functools.partial(spread_kernel, freqs, groups, operator i...]
    all_to_all x7 -> x0, waiting for transfers between devices: 248 us -> none  [the longest x1 82.7 us: local(): lax.all_to_all(local_spectra, 'freq', split_axis=1, concat_axis=0, tiled=...]
    all_to_all x3 -> x0, blocking collectives: 204 us -> none  [the longest x1 97.3 us: local(): lax.all_to_all(local_spectra, 'freq', split_axis=1, concat_axis=0, tiled=...]
    all_to_all x20 -> x0, local copies, waits for them, and re-layouts: 133 us -> none  [the longest x6 57.6 us: local(): lax.all_to_all(direction_low, 'rcv', split_axis=0, concat_axis=3, tiled=T...]
    dot_general x20 -> x12, matrix products: 250 us -> 127 us  [the longest x8 83.2 us: product(): return jnp.einsum(order, left, right, preferred_element_type=jnp.float32)]
    psum x2, blocking collectives: 172 us -> 77.6 us  [local(): lax.psum((residual_sq, jnp.sum(square)), ('freq', 'rcv'))]
    unnamed x63 -> x23, local copies, waits for them, and re-layouts: 112 us -> 33.1 us
    convert_element_type x7 -> x2, local copies, waits for them, and re-layouts: 84 us -> 17.5 us  [local(): local_spectra = jnp.einsum('kct,nts->kncs', table, primaries.astype(jnp.b...]
  transfers between devices with their start and end apart: 8 -> 0, of which waited for: 5 -> 0; matrix products, arithmetic and copies ran while one was open for 16% -> 0% of each run, Pallas kernels for 0% -> 0%
where the time goes in v1:
time: 937 us; the launch traced here: 927 us
  Pallas kernels  573 us (61%)
  matrix products  127 us (14%)
  local copies, waits for them, and re-layouts  124 us (13%)
  blocking collectives  77.6 us (8%)
  other arithmetic  20.7 us (2%)
    pallas_call x2, Pallas kernels, spread(): pl.pallas_call(functools.partial(spread_kernel, freqs, groups, operator i...  323 us
    pallas_call x2, Pallas kernels, collect(): pl.pallas_call(functools.partial(collect_kernel, freqs, groups, resid is...  250 us
    dot_general x8, matrix products, product(): return jnp.einsum(order, left, right, preferred_element_type=jnp.float32)  83.2 us
    psum x2, blocking collectives, local(): lax.psum((residual_sq, jnp.sum(square)), ('freq', 'rcv'))  77.6 us
    unnamed x23, local copies, waits for them, and re-layouts  33.1 us
    dot_general x2, matrix products, local(): jnp.einsum('kct,kncs->nts', table, total.reshape(frequencies, points, 2,...  29.6 us

profile of v1, /device:TPU:0, one launch (start us, length us, event | category | flops | bytes accessed | tf_op | source)
XLA Modules:
  0.0 927.4 jit_solution(8596969399508924929)
XLA Ops:
  0.6 9.3 multiply_convert_fusion
  9.9 4.6 reshape.149
  14.5 0.0 copy-start.2
  14.5 0.0 copy-start.5
  14.5 3.4 copy.46
  17.9 0.0 copy-done.2
  17.9 0.0 copy-done.5
  18.0 8.1 convert_bitcast_fusion.1
  26.0 6.3 copy.18
  32.4 7.6 reshape.129.refs_0_
  40.0 9.2 copy.23
  49.3 206.2 %shard_map.59 = (bf16[32,512,256]{2,1,0:T(8,128)(2,1)}, bf16[32,2,192,512]{3,2,1,0:T(8,128)(2,1)}, bf16[32,192,256]{2,1,0:T(8,128)(2,1)S(1)}) custom-call(bf16[16,512,256]{2,1,0:T(8,128)(2,1)} %reshape.129.refs_0_, bf16[64,2,96,512]{3,2,1,0:T(8,128)(2,1)} %refs_1_.1, bf16[2,32,96,256]{3,2,1,0:T(8,128)(2,1)} %bitcast.116), custom_call_target="tpu_custom_call" | custom-call | tf_op jit(solution)/shard_map/pallas_call | solution.py:262
  255.5 7.7 copy.20
  263.2 4.2 slice_multiply_fusion.1
  267.5 7.3 fusion
  274.7 9.7 %multiply_reduce_fusion.1 = (f32[]{:T(128)}, bf16[32,192,256]{2,1,0:T(8,128)(2,1)S(1)}) fusion(f32[32,192,256]{2,1,0:T(8,128)} %fusion, bf16[32,512,256]{2,1,0:T(8,128)(2,1)} %bitcast.109, bf16[32,2,192,512]{3,2,1,0:T(8,128)(2,1)} %get-tuple-element.11, bf16[32,192,256]{2,1,0:T(8,128)(2,1)S(1)} %get-tuple-element.10), kind=kOutput, calls=%fused_computation.33 | convolution fusion | flops 1621622784 | bytes 27262980 | tf_op jit(solution)/shard_map/krn,kns->krs/dot_general | solution.py:374
  284.4 1.9 fusion.75
  286.3 11.1 %fusion.18 = f32[32,512,256]{2,1,0:T(8,128)} fusion(bf16[32,192,256]{2,1,0:T(8,128)(2,1)S(1)} %get-tuple-element.39, bf16[32,2,192,512]{3,2,1,0:T(8,128)(2,1)} %get-tuple-element.11), kind=kOutput, calls=%fused_computation.28 | convolution fusion | flops 1610612736 | bytes 26214400 | tf_op jit(solution)/shard_map/krn,krs->kns/dot_general | solution.py:374
  297.4 13.6 %add_convert_fusion.1 = bf16[32,512,256]{2,1,0:T(8,128)(2,1)} fusion(f32[32,512,256]{2,1,0:T(8,128)} %fusion.18, bf16[32,2,192,512]{3,2,1,0:T(8,128)(2,1)} %get-tuple-element.11, bf16[32,192,128]{2,1,0:T(8,128)(2,1)} %get-tuple-element.37, bf16[32,192,128]{2,1,0:T(8,128)(2,1)} %get-tuple-element.36), kind=kOutput, calls=%fused_computation.1 | convolution fusion | flops 1625292800 | bytes 34603008 | tf_op jit(solution)/shard_map/krn,krs->kns/dot_general | solution.py:374
  311.1 7.7 copy.21
  318.8 0.0 copy-start.8
  318.8 114.7 %shard_map.60 = (bf16[16,512,256]{2,1,0:T(8,128)(2,1)S(1)}, f32[8,256]{1,0:T(8,128)S(1)}) custom-call(bf16[32,512,256]{2,1,0:T(8,128)(2,1)} %bitcast.112), custom_call_target="tpu_custom_call" | custom-call | tf_op jit(solution)/shard_map/pallas_call | solution.py:297
  433.5 0.0 copy-start.1
  433.5 1.9 copy-done.1
  435.4 0.6 reduce_sum.37
  436.0 38.0 %all-reduce.1 = (f32[]{:T(128)}, f32[]{:T(128)}) all-reduce(f32[]{:T(128)} %get-tuple-element.38, f32[]{:T(128)} %reduce_sum.37), channel_id=1, replica_groups=mesh['freq'=8,'rcv'=4] {'freq','rcv'}, use_global_device_ids=true, to_apply=%region_1.2 | all-reduce | flops 2 | bytes 16 | tf_op jit(solution)/shard_map/psum | solution.py:347
  475.9 0.0 copy-done.8
  475.9 7.0 reshape.135
  482.9 0.0 copy-start.3
  482.9 0.0 copy-start.6
  482.9 13.5 %minimum_subtract_fusion.1 = f32[16,1024,128]{1,2,0:T(8,128)S(1)} fusion(f32[16,1024,128]{1,2,0:T(8,128)} %copy.23, f32[128]{0:T(128)S(1)} %get-tuple-element.28, f32[128]{0:T(128)S(1)} %get-tuple-element.29, f32[]{:T(128)S(6)} %div.12, bf16[512,16,2,128]{3,2,1,0:T(2,128)(2,1)} %reshape.135, bf16[512,1,1024]{2,0,1:T(8,128)(2,1)} %get-tuple-element.42, ...), kind=kOutput, calls=%fused_computation.15 | convolution fusion | flops 4306501632 | bytes 23069700 | tf_op jit(solution)/shard_map/kct,kncs->nts/dot_general | solution.py:352
  496.4 0.0 copy-start.9
  496.4 3.4 copy-done.9
  499.8 0.0 copy-done.3
  499.8 0.0 copy-done.6
  499.8 6.2 convert_bitcast_fusion
  505.9 11.2 %copy.24 = bf16[512,16,2,128]{3,2,1,0:T(2,128)(2,1)} copy(bf16[512,16,2,128]{0,3,2,1:T(8,128)(2,1)} %convert_bitcast_fusion) | data formatting | bytes 8388608 | tf_op jit(solution)/shard_map/convert_element_type | solution.py:329
  517.2 7.8 reshape.136.refs_0_
  525.0 0.0 copy-start
  525.0 2.2 copy-done
  527.2 116.9 %shard_map.61 = bf16[32,512,256]{2,1,0:T(8,128)(2,1)} custom-call(bf16[16,512,256]{2,1,0:T(8,128)(2,1)S(1)} %copy-done), custom_call_target="tpu_custom_call" | custom-call | tf_op jit(solution)/shard_map/pallas_call | solution.py:262
  644.1 7.7 copy.25
  651.9 3.8 slice_multiply_fusion
  655.6 7.3 fusion.4
  662.9 9.7 %multiply_reduce_fusion = (f32[]{:T(128)}, bf16[32,192,256]{2,1,0:T(8,128)(2,1)S(1)}) fusion(f32[32,192,256]{2,1,0:T(8,128)} %fusion.4, bf16[32,512,256]{2,1,0:T(8,128)(2,1)} %bitcast.107, bf16[32,2,192,512]{3,2,1,0:T(8,128)(2,1)} %get-tuple-element.11, bf16[32,192,256]{2,1,0:T(8,128)(2,1)S(1)} %get-tuple-element.10), kind=kOutput, calls=%fused_computation.32 | convolution fusion | flops 1621622784 | bytes 27262980 | tf_op jit(solution)/shard_map/krn,kns->krs/dot_general | solution.py:374
  672.6 1.9 copy.47
  674.5 0.3 fusion.74
  674.7 11.1 %fusion.14 = f32[32,512,256]{2,1,0:T(8,128)} fusion(bf16[32,192,256]{2,1,0:T(8,128)(2,1)S(1)} %get-tuple-element.41, bf16[32,2,192,512]{3,2,1,0:T(8,128)(2,1)} %get-tuple-element.11), kind=kOutput, calls=%fused_computation.24 | convolution fusion | flops 1610612736 | bytes 26214400 | tf_op jit(solution)/shard_map/krn,krs->kns/dot_general | solution.py:374
  685.8 13.4 %add_convert_fusion = bf16[32,512,256]{2,1,0:T(8,128)(2,1)} fusion(f32[32,512,256]{2,1,0:T(8,128)} %fusion.14, bf16[32,2,192,512]{3,2,1,0:T(8,128)(2,1)} %get-tuple-element.11, bf16[32,192,128]{2,1,0:T(8,128)(2,1)S(1)} %get-tuple-element.35, bf16[32,192,128]{2,1,0:T(8,128)(2,1)S(1)} %get-tuple-element.34), kind=kOutput, calls=%fused_computation | convolution fusion | flops 1625292800 | bytes 34603008 | tf_op jit(solution)/shard_map/krn,krs->kns/dot_general | solution.py:374
  699.3 7.7 copy.26
  707.0 135.0 %shard_map.62 = (bf16[16,512,256]{2,1,0:T(8,128)(2,1)}, f32[8,256]{1,0:T(8,128)S(1)}, bf16[64,96,256]{2,1,0:T(8,128)(2,1)S(1)}) custom-call(bf16[32,512,256]{2,1,0:T(8,128)(2,1)} %bitcast.111, bf16[2,32,96,256]{3,2,1,0:T(8,128)(2,1)} %bitcast.117), custom_call_target="tpu_custom_call" | custom-call | tf_op jit(solution)/shard_map/pallas_call | solution.py:297
  842.1 0.6 reduce_sum.39
  842.7 39.6 %all-reduce = (f32[]{:T(128)}, f32[]{:T(128)}) all-reduce(f32[]{:T(128)} %get-tuple-element.40, f32[]{:T(128)} %reduce_sum.39), channel_id=1, replica_groups=mesh['freq'=8,'rcv'=4] {'freq','rcv'}, use_global_device_ids=true, to_apply=%region_5.6 | all-reduce | flops 2 | bytes 16 | tf_op jit(solution)/shard_map/psum | solution.py:347
  884.3 3.0 reshape.143
  887.4 7.1 copy.30
  894.4 0.0 copy-start.4
  894.4 0.0 copy-start.7
  894.5 7.1 reshape.142
  901.5 0.0 copy-done.4
  901.5 0.0 copy-done.7
  901.5 16.2 %minimum_subtract_fusion = f32[16,1024,128]{1,2,0:T(8,128)} fusion(f32[16,1024,128]{1,2,0:T(8,128)} %copy-done.9, f32[128]{0:T(128)S(1)} %get-tuple-element.26, f32[128]{0:T(128)S(1)} %get-tuple-element.27, f32[]{:T(128)S(6)} %div.14, bf16[512,16,2,128]{3,2,1,0:T(2,128)(2,1)} %reshape.142, bf16[512,1,1024]{2,0,1:T(8,128)(2,1)S(1)} %copy-done.4, ...), kind=kOutput, calls=%fused_computation.14 | convolution fusion | flops 4306501632 | bytes 23069700 | tf_op jit(solution)/shard_map/kct,kncs->nts/dot_general | solution.py:352
  917.7 9.2 copy.29
  (2 shorter events, 0.0 us)
Async XLA Ops:
  14.5 3.5 copy-start.2
  14.5 3.5 copy-start.5
  318.8 157.1 %copy-start.8 = (f32[128]{0:T(128)S(1)}, f32[128]{0:T(128)}, u32[]{:S(2)}) copy-start(f32[128]{0:T(128)} %param.7) | copy-start | bytes 1540
  433.5 1.9 copy-start.1
  482.9 16.9 %copy-start.3 = (bf16[512,1,1024]{2,0,1:T(8,128)(2,1)S(1)}, bf16[512,1,1024]{2,0,1:T(8,128)(2,1)}, u32[]{:S(2)}) copy-start(bf16[512,1,1024]{2,0,1:T(8,128)(2,1)} %get-tuple-element.42) | copy-start | bytes 3145732
  482.9 16.9 %copy-start.6 = (bf16[512,1,1024]{2,0,1:T(8,128)(2,1)S(1)}, bf16[512,1,1024]{2,0,1:T(8,128)(2,1)}, u32[]{:S(2)}) copy-start(bf16[512,1,1024]{2,0,1:T(8,128)(2,1)} %get-tuple-element.43) | copy-start | bytes 3145732
  496.4 3.4 copy-start.9
  525.0 2.2 copy-start
  894.4 7.1 copy-start.4
  894.4 7.1 copy-start.7

commit v2 on v1

--- a/solution.py
+++ b/solution.py
@@ -3,6 +3,7 @@
 
 import jax
 import jax.numpy as jnp
+import numpy as np
 from jax import lax
 from jax.experimental import pallas as pl
 from jax.experimental.pallas import tpu as pltpu
@@ -10,19 +11,17 @@
 
 ITERS = 2
 CORES = 2
+SWAPS = 8
 MESH = pl.DeviceIdType.MESH
-VMEM_LIMIT = 48 * 1024 * 1024
+VMEM_LIMIT = 56 * 1024 * 1024
 
 
 def transform_table(frequencies, samples):
-    freq_index = jnp.arange(frequencies, dtype=jnp.int32)[:, None]
-    sample_index = jnp.arange(samples, dtype=jnp.int32)[None, :]
-    phase = freq_index * sample_index % samples
-    angle = phase.astype(jnp.float32) * (2.0 * math.pi / samples)
+    phase = np.arange(frequencies)[:, None] * np.arange(samples)[None, :] % samples
+    angle = phase * (2.0 * math.pi / samples)
     factor = math.sqrt(2.0 / samples)
-    return jnp.stack([factor * jnp.cos(angle), -factor * jnp.sin(angle)], axis=1).astype(
-        jnp.bfloat16
-    )
+    rows = np.concatenate([factor * np.cos(angle), -factor * np.sin(angle)], axis=0)
+    return rows.astype(np.float32).astype(jnp.bfloat16)
 
 
 def place(groups):
@@ -104,19 +103,17 @@
     others = []
     if with_operator:
         sibling = 1 - core
-        held = oper.shape[2]
-        rows = pl.ds(pl.multiple_of(core * held, 16), held)
         kept = oper_out.shape[0]
-        for number, (source, target, first) in enumerate(
-            [
+        size = kept // SWAPS
+        pieces = [(data.at[sibling], data_out)]
+        for piece in range(SWAPS):
+            pieces.append(
                 (
-                    oper.at[pl.ds(sibling * kept, kept)],
-                    oper_out.at[:, :, rows, :],
-                    oper.at[pl.ds(core * kept, kept)],
-                ),
-                (data.at[sibling], data_out.at[:, rows, :], data.at[core]),
-            ]
-        ):
+                    oper.at[pl.ds(sibling * kept + piece * size, size)],
+                    oper_out.at[pl.ds(piece * size, size)],
+                )
+            )
+        for number, (source, target) in enumerate(pieces):
             away = pltpu.make_async_remote_copy(
                 src_ref=source,
                 dst_ref=target,
@@ -126,9 +123,7 @@
                 device_id_type=MESH,
             )
             away.start()
-            here = pltpu.make_async_copy(first, target, local.at[1 + number])
-            here.start()
-            others += [away, here]
+            others.append(away)
     for offset in order:
         direct(offset).wait_recv()
         for hop in range(1, groups):
@@ -145,10 +140,12 @@
 
 def collect_kernel(freqs, groups, with_residual, *refs):
     if with_residual:
-        part, resid, total, square, resid_out, landed, ready, mine, *sems = refs
-        send, recv, send_y, recv_y, local, swap_send, swap_recv = sems
+        part, resid_sq, resid, resid_away, total, norms, resid_out, *rest = refs
+        *rest, swap_send, swap_recv = rest
     else:
-        part, total, square, landed, ready, mine, send, recv, send_y, recv_y, local = refs
+        part, resid_sq, total, norms, *rest = refs
+    landed, ready, mine, sums, sums_y, sums_all, *rest = rest
+    send, recv, send_y, recv_y, local, norm_send, norm_recv = rest
     freq, group, core = place(groups)
     count = freqs * CORES
     rows = part.shape[1]
@@ -195,11 +192,9 @@
         fetch(offset).start()
     if with_residual:
         sibling = 1 - core
-        held = resid.shape[2]
-        kept = resid.shape[1]
-        rows_of = resid_out.shape[0] // CORES
+        kept = resid.shape[0]
         away = pltpu.make_async_remote_copy(
-            src_ref=resid.at[sibling],
+            src_ref=resid_away,
             dst_ref=resid_out.at[pl.ds(core * kept, kept)],
             send_sem=swap_send.at[0],
             recv_sem=swap_recv.at[0],
@@ -208,11 +203,12 @@
         )
         away.start()
         here = pltpu.make_async_copy(
-            resid.at[core], resid_out.at[pl.ds(core * kept, kept)], local.at[count]
+            resid, resid_out.at[pl.ds(core * kept, kept)], local.at[count]
         )
         here.start()
         others = [away, here]
-    square[...] = jnp.zeros_like(square)
+    sums[0] = resid_sq[...]
+    sums[1] = jnp.zeros_like(resid_sq)
     tile = min(rows, 128)
     for offset in order:
         fetch(offset).wait()
@@ -226,12 +222,47 @@
             for hop in range(1, groups):
                 value += landed[(hop - 1) * count + offset, here, :].astype(jnp.float32)
             ready[offset, here, :] = value.astype(jnp.bfloat16)
-            square[...] += jnp.sum((value * value).reshape(tile // 8, 8, -1), axis=0)
+            sums[1] += jnp.sum((value * value).reshape(tile // 8, 8, -1), axis=0)
 
         if offset:
             direct(offset).start()
+    def norm_across(hop):
+        there = lax.rem(group + hop, groups)
+        return pltpu.make_async_remote_copy(
+            src_ref=sums,
+            dst_ref=sums_y.at[hop - 1],
+            send_sem=norm_send.at[count + hop - 1],
+            recv_sem=norm_recv.at[count + hop - 1],
+            device_id=(freq, there * CORES + core),
+            device_id_type=MESH,
+        )
+
+    def norm_direct(offset):
+        to_freq, _, other = peers_of(freqs, offset, freq, core)
+        return pltpu.make_async_remote_copy(
+            src_ref=sums_all.at[0],
+            dst_ref=sums_all.at[offset],
+            send_sem=norm_send.at[offset],
+            recv_sem=norm_recv.at[offset],
+            device_id=(to_freq, group * CORES + other),
+            device_id_type=MESH,
+        )
+
+    for hop in range(1, groups):
+        norm_across(hop).start()
     last = pltpu.make_async_copy(ready.at[0], total.at[freq * CORES + core], local.at[count + 1])
     last.start()
+    value = sums[...]
+    for hop in range(1, groups):
+        norm_across(hop).wait()
+        value = value + sums_y[hop - 1]
+    sums_all[0] = value
+    for offset in range(1, count):
+        norm_direct(offset).start()
+    for offset in range(1, count):
+        norm_direct(offset).wait()
+        value = value + sums_all[offset]
+    norms[...] = value
     last.wait()
     for offset in range(1, count):
         direct(offset).wait()
@@ -253,10 +284,10 @@
         kb, two, held, points = operator.shape
         _, kept, _, width = data.shape
         shapes += [
-            jax.ShapeDtypeStruct((kb // CORES, two, held * CORES, points), jnp.bfloat16),
-            jax.ShapeDtypeStruct((kept, held * CORES, width), jnp.bfloat16),
+            jax.ShapeDtypeStruct((kb // CORES, two, held, points), jnp.bfloat16),
+            jax.ShapeDtypeStruct((kept, held, width), jnp.bfloat16),
         ]
-        sems += [dma((2,)), dma((2,))]
+        sems += [dma((SWAPS + 1,)), dma((SWAPS + 1,))]
         args += [operator, data]
     anywhere = pl.BlockSpec(memory_space=pl.ANY)
     return pl.pallas_call(
@@ -271,39 +302,290 @@
     )(*args)
 
 
-def collect(freqs, groups, ident, part, resid=None):
+def collect(freqs, groups, ident, part, resid_sq, resid=None, resid_away=None):
     count = freqs * CORES
     _, rows, width = part.shape
     dma = pltpu.SemaphoreType.DMA
+    pair = (2,) + resid_sq.shape
     shapes = [
         jax.ShapeDtypeStruct((count, rows, width), jnp.bfloat16),
-        jax.ShapeDtypeStruct((8, width), jnp.float32),
+        jax.ShapeDtypeStruct(pair, jnp.float32),
     ]
     scratch = [
         pltpu.VMEM(((groups - 1) * count, rows, width), jnp.bfloat16),
         pltpu.VMEM((count, rows, width), jnp.bfloat16),
         pltpu.VMEM((count, rows, width), jnp.bfloat16),
+        pltpu.VMEM(pair, jnp.float32),
+        pltpu.VMEM((groups - 1,) + pair, jnp.float32),
+        pltpu.VMEM((count,) + pair, jnp.float32),
         dma((count,)), dma((count,)), dma(((groups - 1) * count,)), dma(((groups - 1) * count,)), dma((count + 2,)),
+        dma((count + groups - 1,)), dma((count + groups - 1,)),
     ]
     anywhere = pl.BlockSpec(memory_space=pl.ANY)
     outs = [anywhere, pl.BlockSpec(memory_space=pltpu.VMEM)]
-    args = [part]
+    args = [part, resid_sq]
     if resid is not None:
-        _, kept, held, _ = resid.shape
+        kept, held, _ = resid.shape
         shapes.append(jax.ShapeDtypeStruct((kept * CORES, held, width), jnp.bfloat16))
         outs.append(anywhere)
         scratch += [dma((1,)), dma((1,))]
-        args.append(resid)
+        args += [resid, resid_away]
     return pl.pallas_call(
         functools.partial(collect_kernel, freqs, groups, resid is not None),
         out_shape=shapes,
-        in_specs=[anywhere] * len(args),
+        in_specs=[anywhere, pl.BlockSpec(memory_space=pltpu.VMEM)] + [anywhere] * (len(args) - 2),
         out_specs=outs,
         scratch_shapes=scratch,
         compiler_params=pltpu.CompilerParams(
             collective_id=ident, has_side_effects=True, vmem_limit_bytes=VMEM_LIMIT
         ),
     )(*args)
+
+
+def interleave(value, scratch, point, sources, frequencies):
+    stride = scratch[0].shape[0] // frequencies
+    for which in range(2):
+        for part in range(2):
+            scratch[part][pl.ds(point + which, frequencies, stride=stride), :] = value[
+                part * frequencies : (part + 1) * frequencies,
+                which * sources : (which + 1) * sources,
+            ]
+
+
+def write_out(out, scratch, sources):
+    tile = 1024
+
+    @pl.loop(0, out.shape[0] // tile)
+    def write(step):
+        rows = pl.ds(pl.multiple_of(step * tile, tile), tile)
+        for part in range(2):
+            out[rows, part * sources : (part + 1) * sources] = scratch[part][rows, :].astype(
+                jnp.bfloat16
+            )
+
+
+def pair_of(prim):
+    return jnp.concatenate([prim[0], prim[1]], axis=1)
+
+
+def forward_kernel(prim, table, out, *scratch):
+    sources = prim.shape[2]
+    frequencies = table.shape[0] // 2
+    step = pl.program_id(0)
+    value = jnp.dot(
+        table[...], pair_of(prim).astype(jnp.bfloat16), preferred_element_type=jnp.float32
+    )
+    interleave(value, scratch, 2 * step, sources, frequencies)
+
+    @pl.when(step == pl.num_programs(0) - 1)
+    def finish():
+        write_out(out, scratch, sources)
+
+
+def update_kernel(count_total, last, *refs):
+    if last:
+        norms, shrink, total, prim, turned_table, prim_out, real, imag = refs
+    else:
+        norms, shrink, total, prim, turned_table, table, prim_out, out, real, imag, *scratch = refs
+    sources = prim.shape[2]
+    frequencies = turned_table.shape[1] // 2
+    stride = total.shape[0] // frequencies
+    step = pl.program_id(0)
+    tile = 1024
+
+    @pl.when(step == 0)
+    def widen():
+        @pl.loop(0, total.shape[0] // tile)
+        def copy(step):
+            rows = pl.ds(pl.multiple_of(step * tile, tile), tile)
+            real[rows, :] = total[rows, :sources].astype(jnp.float32)
+            imag[rows, :] = total[rows, sources:].astype(jnp.float32)
+
+    residual_norm = jnp.sum(norms[0], axis=(0, 1), keepdims=True)
+    direction_norm = jnp.sum(norms[1], axis=(0, 1), keepdims=True)
+    step_size = 0.5 * residual_norm / (direction_norm + 1e-06)
+    threshold = shrink[...] * (step_size * jnp.sqrt(direction_norm / count_total))
+    threshold = jnp.concatenate([threshold, threshold], axis=1)
+
+    def column(point):
+        rows = pl.ds(point, frequencies, stride=stride)
+        return jnp.concatenate([real[rows, :], imag[rows, :]], axis=0).astype(jnp.bfloat16)
+
+    both = jnp.concatenate([column(2 * step), column(2 * step + 1)], axis=1)
+    update = jnp.dot(turned_table[...], both, preferred_element_type=jnp.float32)
+    moved = pair_of(prim) + step_size * update
+    fresh = moved - jnp.clip(moved, -threshold, threshold)
+    prim_out[0] = fresh[:, :sources]
+    prim_out[1] = fresh[:, sources:]
+    if last:
+        return
+    value = jnp.dot(table[...], fresh.astype(jnp.bfloat16), preferred_element_type=jnp.float32)
+    interleave(value, scratch, 2 * step, sources, frequencies)
+
+    @pl.when(step == pl.num_programs(0) - 1)
+    def finish():
+        write_out(out, scratch, sources)
+
+
+def products_kernel(core_ref, near, far, spectra, near_data, far_data, near_res, far_res, part, square):
+    held = near.shape[2]
+    points = spectra.shape[0] * spectra.shape[2]
+    width = spectra.shape[3]
+    sources = width // 2
+    values = spectra[...].reshape(points, width)
+    real_op = jnp.concatenate([near[0, 0], far[0, 0]], axis=0)
+    imag_op = jnp.concatenate([near[0, 1], far[0, 1]], axis=0)
+
+    def product(left, right, side):
+        return lax.dot_general(
+            left, right, (((side,), (0,)), ((), ())), preferred_element_type=jnp.float32
+        )
+
+    def turned(values):
+        return jnp.concatenate([-values[:, sources:], values[:, :sources]], axis=1)
+
+    predicted = product(real_op, values, 1) + product(imag_op, turned(values), 1)
+    recorded = jnp.concatenate([near_data[0, 0], far_data[0]], axis=0).astype(jnp.float32)
+    resid = (recorded - predicted).astype(jnp.bfloat16)
+    near_res[0] = resid[:held]
+    far_res[0] = resid[held:]
+
+    @pl.when(pl.program_id(0) == 0)
+    def clear():
+        square[...] = jnp.zeros_like(square)
+
+    wide = resid.astype(jnp.float32)
+    square[...] += jnp.sum((wide * wide).reshape(-1, 8, width), axis=0)
+    direction = product(real_op, resid, 0) - product(imag_op, turned(resid), 0)
+    part[...] = direction.astype(jnp.bfloat16).reshape(part.shape)
+
+
+def params():
+    return pltpu.CompilerParams(vmem_limit_bytes=VMEM_LIMIT)
+
+
+def once(shape):
+    return pl.BlockSpec(shape, lambda *_: (0,) * len(shape), pipeline_mode=pl.Buffered(1))
+
+
+def forward(prim, table):
+    points, samples, sources = prim.shape
+    rows = table.shape[0] // 2 * points
+    return pl.pallas_call(
+        forward_kernel,
+        grid=(points // 2,),
+        out_shape=jax.ShapeDtypeStruct((rows, 2 * sources), jnp.bfloat16),
+        in_specs=[pl.BlockSpec((2, samples, sources), lambda i: (i, 0, 0)), once(table.shape)],
+        out_specs=once((rows, 2 * sources)),
+        scratch_shapes=[pltpu.VMEM((rows, sources), jnp.float32)] * 2,
+        compiler_params=params(),
+    )(prim, table)
+
+
+def advance(norms, shrink, total, prim, turned_table, table, count_total, last):
+    points, samples, sources = prim.shape
+    rows = total.shape[0]
+    block = pl.BlockSpec((2, samples, sources), lambda i: (i, 0, 0))
+    args = [norms, shrink, total, prim, turned_table]
+    specs = [once(norms.shape), once(shrink.shape), once(total.shape), block, once(turned_table.shape)]
+    shapes, outs = [jax.ShapeDtypeStruct(prim.shape, jnp.float32)], [block]
+    scratch = [pltpu.VMEM((rows, sources), jnp.float32)] * (2 if last else 4)
+    if not last:
+        args.append(table)
+        specs.append(once(table.shape))
+        shapes.append(jax.ShapeDtypeStruct(total.shape, jnp.bfloat16))
+        outs.append(once(total.shape))
+    return pl.pallas_call(
+        functools.partial(update_kernel, count_total, last),
+        grid=(points // 2,),
+        out_shape=shapes,
+        in_specs=specs,
+        out_specs=outs,
+        scratch_shapes=scratch,
+        compiler_params=params(),
+    )(*args)
+
+
+def products(core, near, far, spectra, near_data, far_data):
+    kept, _, held, _ = far.shape
+    everywhere, _, points, width = spectra.shape
+    rows = pl.BlockSpec((1, held, width), lambda k, c: (k, 0, 0))
+    spread_block = pl.BlockSpec((everywhere, 1, points, width), lambda k, c: (0, k, 0, 0))
+    resid_shape = jax.ShapeDtypeStruct((kept, held, width), jnp.bfloat16)
+    return pl.pallas_call(
+        products_kernel,
+        grid_spec=pltpu.PrefetchScalarGridSpec(
+            num_scalar_prefetch=1,
+            grid=(kept,),
+            in_specs=[
+                pl.BlockSpec((1,) + far.shape[1:], lambda k, c: (c[0] * kept + k, 0, 0, 0)),
+                pl.BlockSpec((1,) + far.shape[1:], lambda k, c: (k, 0, 0, 0)),
+                spread_block,
+                pl.BlockSpec((1, 1, held, width), lambda k, c: (c[0], k, 0, 0)),
+                rows,
+            ],
+            out_specs=[rows, rows, spread_block, pl.BlockSpec((8, width), lambda k, c: (0, 0))],
+        ),
+        out_shape=[
+            resid_shape,
+            resid_shape,
+            jax.ShapeDtypeStruct(spectra.shape, jnp.bfloat16),
+            jax.ShapeDtypeStruct((8, width), jnp.float32),
+        ],
+        compiler_params=params(),
+    )(core, near, far, spectra, near_data, far_data)
+
+
+def plain_forward(prim, table):
+    points, samples, sources = prim.shape
+    spectra = jnp.einsum(
+        "ckt,nts->kncs",
+        table.reshape(2, -1, samples),
+        prim.astype(jnp.bfloat16),
+        preferred_element_type=jnp.float32,
+    ).astype(jnp.bfloat16)
+    return spectra.reshape(-1, 2 * sources)
+
+
+def plain_advance(norms, shrink, total, prim, turned_table, table, count_total, last):
+    points, samples, sources = prim.shape
+    residual_norm, direction_norm = jnp.sum(norms[0]), jnp.sum(norms[1])
+    step_size = 0.5 * residual_norm / (direction_norm + 1e-06)
+    threshold = shrink[:, None, :] * (step_size * jnp.sqrt(direction_norm / count_total))
+    update = jnp.einsum(
+        "ckt,kncs->nts",
+        table.reshape(2, -1, samples),
+        total.reshape(-1, points, 2, sources),
+        preferred_element_type=jnp.float32,
+    )
+    moved = prim + step_size * update
+    fresh = moved - jnp.clip(moved, -threshold, threshold)
+    return (fresh,) if last else (fresh, plain_forward(fresh, table))
+
+
+def plain_products(core, near, far, spectra, near_data, far_data):
+    kept, _, held, _ = far.shape
+    everywhere, _, points, width = spectra.shape
+    sources = width // 2
+    near = lax.dynamic_slice_in_dim(near, core[0] * kept, kept, 0)
+    operator = jnp.concatenate([near, far], axis=2)
+    near_data = lax.dynamic_index_in_dim(near_data, core[0], 0, keepdims=False)
+    recorded = jnp.concatenate([near_data, far_data], axis=1)
+    values = spectra.transpose(1, 0, 2, 3).reshape(kept, everywhere * points, width)
+
+    def turned(values):
+        return jnp.concatenate([-values[:, :, sources:], values[:, :, :sources]], axis=2)
+
+    def product(order, part, right):
+        return jnp.einsum(order, operator[:, part], right, preferred_element_type=jnp.float32)
+
+    ahead, back = "krn,kns->krs", "krn,krs->kns"
+    predicted = product(ahead, 0, values) + product(ahead, 1, turned(values))
+    resid = (recorded.astype(jnp.float32) - predicted).astype(jnp.bfloat16)
+    square = jnp.sum(jnp.square(resid.astype(jnp.float32)).reshape(-1, 8, width), axis=0)
+    direction = product(back, 0, resid) - product(back, 1, turned(resid))
+    part = direction.astype(jnp.bfloat16).reshape(kept, everywhere, points, width)
+    return resid[:, :held], resid[:, held:], part.transpose(1, 0, 2, 3), square
 
 
 def local(freqs, groups, primaries_start, surface_operator, data_spectra, shrinkage):
@@ -314,71 +596,49 @@
     everywhere = groups * count
     frequencies = band * freqs
     width = 2 * sources
-    table = transform_table(frequencies, samples)
+    rows = transform_table(frequencies, samples)
+    table, turned_table = jnp.asarray(rows), jnp.asarray(np.ascontiguousarray(rows.T))
     primaries = primaries_start
     count_total = 2.0 * frequencies * all_points * sources
-
+    whole_tiles = points % 16 == 0
+    go_forward, go_advance, multiply = (
+        (forward, advance, products)
+        if whole_tiles
+        else (plain_forward, plain_advance, plain_products)
+    )
+
+    core = lax.rem(lax.axis_index("rcv"), CORES).astype(jnp.int32).reshape(1)
     data = data_spectra.reshape(held, CORES, kept, width).transpose(1, 2, 0, 3)
-    operator = recorded = None
+    shrink = shrinkage.reshape(1, sources)
+    local_spectra = go_forward(primaries, table)
     for iteration in range(ITERS):
-        local_spectra = jnp.einsum(
-            "kct,nts->kncs",
-            table,
-            primaries.astype(jnp.bfloat16),
-            preferred_element_type=jnp.float32,
-        ).astype(jnp.bfloat16).reshape(count, kept * points, width)
+        last = iteration == ITERS - 1
+        message = local_spectra.reshape(count, kept * points, width)
         if iteration == 0:
-            spectra, operator, recorded = spread(
-                freqs, groups, 0, local_spectra, surface_operator, data
-            )
+            spectra, far, far_data = spread(freqs, groups, 0, message, surface_operator, data)
         else:
-            (spectra,) = spread(freqs, groups, 2, local_spectra)
-        spectra = spectra.reshape(everywhere, kept, points, width).transpose(1, 0, 2, 3)
-        spectra = spectra.reshape(kept, all_points, width)
-        resid, direction = products(operator, spectra, recorded)
-        residual_sq = jnp.sum(jnp.square(resid.astype(jnp.float32)))
-        part = direction.reshape(kept, everywhere, points, width).transpose(1, 0, 2, 3)
+            (spectra,) = spread(freqs, groups, 2, message)
+        near_res, far_res, part, square = multiply(
+            core,
+            surface_operator,
+            far,
+            spectra.reshape(everywhere, kept, points, width),
+            data,
+            far_data,
+        )
         part = part.reshape(everywhere, kept * points, width)
-        if iteration < ITERS - 1:
-            total, square = collect(freqs, groups, 1, part)
+        if not last:
+            total, norms = collect(freqs, groups, 1, part, square)
         else:
-            halves = resid.reshape(kept, CORES, held, width).transpose(1, 0, 2, 3)
-            total, square, residual = collect(freqs, groups, 3, part, halves)
-        residual_norm, direction_norm = lax.psum(
-            (residual_sq, jnp.sum(square)), ("freq", "rcv")
-        )
-        step_size = 0.5 * residual_norm / (direction_norm + 1e-06)
-        threshold = shrinkage[None, None, :] * (step_size * jnp.sqrt(direction_norm / count_total))
-        update = jnp.einsum(
-            "kct,kncs->nts",
-            table,
-            total.reshape(frequencies, points, 2, sources),
-            preferred_element_type=jnp.float32,
-        )
-        moved = primaries + step_size * update
-        primaries = moved - jnp.clip(moved, -threshold, threshold)
+            total, norms, residual = collect(freqs, groups, 3, part, square, near_res, far_res)
+        total = total.reshape(frequencies * points, width)
+        primaries, *more = go_advance(
+            norms, shrink, total, primaries, turned_table, table, count_total, last
+        )
+        if more:
+            (local_spectra,) = more
     residual = residual.transpose(1, 0, 2).reshape(held, band, 2, sources)
     return (primaries, residual)
-
-
-def products(operator, spectra, recorded):
-    sources = spectra.shape[2] // 2
-    real_op, imag_op = operator[:, 0], operator[:, 1]
-
-    def turned(values, sign):
-        return jnp.concatenate(
-            [-sign * values[:, :, sources:], sign * values[:, :, :sources]], axis=2
-        )
-
-    def product(left, right, order):
-        return jnp.einsum(order, left, right, preferred_element_type=jnp.float32)
-
-    ahead = "krn,kns->krs"
-    back = "krn,krs->kns"
-    predicted = product(real_op, spectra, ahead) + product(imag_op, turned(spectra, 1), ahead)
-    resid = (recorded.astype(jnp.float32) - predicted).astype(jnp.bfloat16)
-    direction = product(real_op, resid, back) + product(imag_op, turned(resid, -1), back)
-    return resid, direction.astype(jnp.bfloat16)
 
 
 def solution(mesh):

time: 937 us -> 662 us (0.71)
  matrix products: 127 us -> 0 us
  local copies, waits for them, and re-layouts: 124 us -> 17 us
  blocking collectives: 77.6 us -> 0 us
  Pallas kernels: 573 us -> 642 us
  other arithmetic: 20.7 us -> 0 us
    dot_general x12 -> x0, matrix products: 127 us -> none  [the longest x8 83.2 us: product(): return jnp.einsum(order, left, right, preferred_element_type=jnp.float32)]
    pallas_call x0 -> x5, Pallas kernels: none -> 123 us  [the longest x2 68.9 us: products(): pl.pallas_call(products_kernel, grid_spec=pltpu.PrefetchScalarGridSpec(nu...]
    pallas_call x2, Pallas kernels: 323 us -> 236 us  [spread(): pl.pallas_call(functools.partial(spread_kernel, freqs, groups, operator i...]
    psum x2 -> x0, blocking collectives: 77.6 us -> none  [local(): lax.psum((residual_sq, jnp.sum(square)), ('freq', 'rcv'))]
    reshape x7 -> x0, local copies, waits for them, and re-layouts: 46.8 us -> none  [the longest x2 15.5 us: local(): local_spectra = jnp.einsum('kct,nts->kncs', table, primaries.astype(jnp.b...]
    pallas_call x2, Pallas kernels: 250 us -> 283 us  [collect(): pl.pallas_call(functools.partial(collect_kernel, freqs, groups, resid is...]
    unnamed x23 -> x1, local copies, waits for them, and re-layouts: 33.1 us -> 5.2 us
    convert_element_type x2 -> x0, local copies, waits for them, and re-layouts: 17.5 us -> none  [local(): local_spectra = jnp.einsum('kct,nts->kncs', table, primaries.astype(jnp.b...]
where the time goes in v2:
time: 662 us; the launch traced here: 659 us
  Pallas kernels  642 us (97%)
  local copies, waits for them, and re-layouts  17 us (3%)
    pallas_call x2, Pallas kernels, collect(): pl.pallas_call(functools.partial(collect_kernel, freqs, groups, resid is...  283 us
    pallas_call x2, Pallas kernels, spread(): pl.pallas_call(functools.partial(spread_kernel, freqs, groups, operator i...  236 us
    pallas_call x2, Pallas kernels, products(): pl.pallas_call(products_kernel, grid_spec=pltpu.PrefetchScalarGridSpec(nu...  68.9 us
    pallas_call x2, Pallas kernels, advance(): pl.pallas_call(functools.partial(update_kernel, count_total, last), grid=...  41.2 us

profile of v2, /device:TPU:0, one launch (start us, length us, event | category | flops | bytes accessed | tf_op | source)
XLA Modules:
  0.0 659.3 jit_solution(1755540059452601643)
XLA Ops:
  0.6 4.6 reshape.52
  5.2 3.4 copy.12
  8.7 12.8 %shard_map.77 = bf16[8192,256]{1,0:T(8,128)(2,1)} custom-call(f32[16,1024,128]{2,1,0:T(8,128)} %refs_3_.1, bf16[1024,1024]{1,0:T(8,128)(2,1)} %constant.13.clone.table.refs_5_), custom_call_target="tpu_custom_call" | custom-call | tf_op jit(solution)/shard_map/pallas_call | solution.py:474
  21.5 118.2 %shard_map.78 = (bf16[32,512,256]{2,1,0:T(8,128)(2,1)}, bf16[32,2,96,512]{3,2,1,0:T(8,128)(2,1)}, bf16[32,96,256]{2,1,0:T(8,128)(2,1)}) custom-call(bf16[16,512,256]{2,1,0:T(8,128)(2,1)} %bitcast.20, bf16[64,2,96,512]{3,2,1,0:T(8,128)(2,1)} %near.3, bf16[2,32,96,256]{3,2,1,0:T(8,128)(2,1)} %bitcast.16), custom_call_target="tpu_custom_call" | custom-call | tf_op jit(solution)/shard_map/pallas_call | solution.py:293
  139.6 34.5 %shard_map.79 = (bf16[32,96,256]{2,1,0:T(8,128)(2,1)}, bf16[32,96,256]{2,1,0:T(8,128)(2,1)}, bf16[32,32,16,256]{3,2,1,0:T(8,128)(2,1)}, f32[8,256]{1,0:T(8,128)}) custom-call(s32[1]{0:T(128)} %bitcast.core_ref, bf16[64,2,96,512]{3,2,1,0:T(8,128)(2,1)} %near.3, bf16[32,2,96,512]{3,2,1,0:T(8,128)(2,1)} %get-tuple-element.18.far, ...), custom_call_target="tpu_custom_call" | custom-call | tf_op jit(solution)/shard_map/pallas_call | solution.py:515
  174.1 141.5 %shard_map.80 = (bf16[16,512,256]{2,1,0:T(8,128)(2,1)}, f32[2,8,256]{2,1,0:T(8,128)}) custom-call(bf16[32,512,256]{2,1,0:T(8,128)(2,1)} %bitcast.22, f32[8,256]{1,0:T(8,128)} %get-tuple-element.22.refs_1_), custom_call_target="tpu_custom_call" | custom-call | tf_op jit(solution)/shard_map/pallas_call | solution.py:333
  315.6 27.0 %shard_map.81 = (f32[16,1024,128]{2,1,0:T(8,128)}, bf16[8192,256]{1,0:T(8,128)(2,1)}) custom-call(f32[2,8,256]{2,1,0:T(8,128)} %get-tuple-element.23.refs_0_, f32[1,128]{1,0:T(1,128)} %bitcast.28, bf16[8192,256]{1,0:T(8,128)(2,1)} %bitcast.26, f32[16,1024,128]{2,1,0:T(8,128)} %refs_3_.1, bf16[1024,1024]{1,0:T(8,128)(2,1)} %constant.14.clone.refs_4_, ...), custom_call_target="tpu_custom_call" | custom-call | tf_op jit(solution)/shard_map/pallas_call | solution.py:498
  342.6 117.6 %shard_map.82 = bf16[32,512,256]{2,1,0:T(8,128)(2,1)} custom-call(bf16[16,512,256]{2,1,0:T(8,128)(2,1)} %bitcast.24), custom_call_target="tpu_custom_call" | custom-call | tf_op jit(solution)/shard_map/pallas_call | solution.py:293
  460.1 34.5 %shard_map.83 = (bf16[32,96,256]{2,1,0:T(8,128)(2,1)}, bf16[32,96,256]{2,1,0:T(8,128)(2,1)}, bf16[32,32,16,256]{3,2,1,0:T(8,128)(2,1)}, f32[8,256]{1,0:T(8,128)}) custom-call(s32[1]{0:T(128)} %bitcast.core_ref, bf16[64,2,96,512]{3,2,1,0:T(8,128)(2,1)} %near.3, bf16[32,2,96,512]{3,2,1,0:T(8,128)(2,1)} %get-tuple-element.18.far, ...), custom_call_target="tpu_custom_call" | custom-call | tf_op jit(solution)/shard_map/pallas_call | solution.py:515
  494.6 141.5 %shard_map.84 = (bf16[16,512,256]{2,1,0:T(8,128)(2,1)}, f32[2,8,256]{2,1,0:T(8,128)}, bf16[64,96,256]{2,1,0:T(8,128)(2,1)}) custom-call(bf16[32,512,256]{2,1,0:T(8,128)(2,1)} %bitcast.21, f32[8,256]{1,0:T(8,128)} %get-tuple-element.27.refs_1_, bf16[32,96,256]{2,1,0:T(8,128)(2,1)} %get-tuple-element.28.refs_2_, bf16[32,96,256]{2,1,0:T(8,128)(2,1)} %get-tuple-element.29.refs_3_), custom_call_target="tpu_custom_call" | custom-call | tf_op jit(solution)/shard_map/pallas_call | solution.py:333
  636.1 14.2 %shard_map.85 = f32[16,1024,128]{2,1,0:T(8,128)} custom-call(f32[2,8,256]{2,1,0:T(8,128)} %get-tuple-element.30.refs_0_, f32[1,128]{1,0:T(1,128)} %bitcast.29, bf16[8192,256]{1,0:T(8,128)(2,1)} %bitcast.25, f32[16,1024,128]{2,1,0:T(8,128)} %get-tuple-element.32.refs_3_, bf16[1024,1024]{1,0:T(8,128)(2,1)} %constant.14.clone.refs_4_), custom_call_target="tpu_custom_call" | custom-call | tf_op jit(solution)/shard_map/pallas_call | solution.py:498
  650.3 3.8 reshape.51
  654.1 5.2 copy.9

commit v3 on v2

--- a/solution.py
+++ b/solution.py
@@ -36,6 +36,21 @@
     from_freq = lax.rem(freq + freqs - step, freqs)
     other = lax.rem(core + flip, CORES)
     return to_freq, from_freq, other
+
+
+def far_first(freqs):
+    steps = sorted(range(freqs), key=lambda step: (abs(step - freqs // 2), step))
+    return [step * CORES + flip for step in steps for flip in range(CORES - 1, -1, -1)]
+
+
+def mixed(freqs):
+    steps = sorted(range(1, freqs), key=lambda step: (abs(step - freqs // 2), step))
+    turn = []
+    while steps:
+        turn.append(steps.pop(0))
+        if steps:
+            turn.append(steps.pop(-1))
+    return [1] + [step * CORES + flip for step in turn for flip in range(CORES)]
 
 
 def enter(freqs, groups, freq, group, core):
@@ -91,7 +106,7 @@
             device_id_type=MESH,
         )
 
-    order = list(range(1, count))
+    order = mixed(freqs)
     for offset in order:
         direct(offset).start()
     own = pltpu.make_async_copy(
@@ -144,7 +159,7 @@
         *rest, swap_send, swap_recv = rest
     else:
         part, resid_sq, total, norms, *rest = refs
-    landed, ready, mine, sums, sums_y, sums_all, *rest = rest
+    landed, ready, mine, sums, small, sums_y, sums_all, *rest = rest
     send, recv, send_y, recv_y, local, norm_send, norm_recv = rest
     freq, group, core = place(groups)
     count = freqs * CORES
@@ -184,7 +199,7 @@
             device_id_type=MESH,
         )
 
-    order = list(range(count - 1, -1, -1))
+    order = far_first(freqs)
     others = []
     for offset in order:
         for hop in range(1, groups):
@@ -229,7 +244,7 @@
     def norm_across(hop):
         there = lax.rem(group + hop, groups)
         return pltpu.make_async_remote_copy(
-            src_ref=sums,
+            src_ref=small,
             dst_ref=sums_y.at[hop - 1],
             send_sem=norm_send.at[count + hop - 1],
             recv_sem=norm_recv.at[count + hop - 1],
@@ -248,11 +263,17 @@
             device_id_type=MESH,
         )
 
+    def folded(value):
+        half = value.shape[1] // 2
+        value = value[:, :half] + value[:, half:]
+        return value[:4] + value[4:]
+
+    small[...] = jnp.concatenate([folded(sums[0]), folded(sums[1])], axis=0)
     for hop in range(1, groups):
         norm_across(hop).start()
     last = pltpu.make_async_copy(ready.at[0], total.at[freq * CORES + core], local.at[count + 1])
     last.start()
-    value = sums[...]
+    value = small[...]
     for hop in range(1, groups):
         norm_across(hop).wait()
         value = value + sums_y[hop - 1]
@@ -307,22 +328,24 @@
     _, rows, width = part.shape
     dma = pltpu.SemaphoreType.DMA
     pair = (2,) + resid_sq.shape
+    packed = (8, width // 2)
     shapes = [
         jax.ShapeDtypeStruct((count, rows, width), jnp.bfloat16),
-        jax.ShapeDtypeStruct(pair, jnp.float32),
+        jax.ShapeDtypeStruct(packed, jnp.float32),
     ]
     scratch = [
         pltpu.VMEM(((groups - 1) * count, rows, width), jnp.bfloat16),
         pltpu.VMEM((count, rows, width), jnp.bfloat16),
         pltpu.VMEM((count, rows, width), jnp.bfloat16),
         pltpu.VMEM(pair, jnp.float32),
-        pltpu.VMEM((groups - 1,) + pair, jnp.float32),
-        pltpu.VMEM((count,) + pair, jnp.float32),
+        pltpu.VMEM(packed, jnp.float32),
+        pltpu.VMEM((groups - 1,) + packed, jnp.float32),
+        pltpu.VMEM((count,) + packed, jnp.float32),
         dma((count,)), dma((count,)), dma(((groups - 1) * count,)), dma(((groups - 1) * count,)), dma((count + 2,)),
         dma((count + groups - 1,)), dma((count + groups - 1,)),
     ]
     anywhere = pl.BlockSpec(memory_space=pl.ANY)
-    outs = [anywhere, pl.BlockSpec(memory_space=pltpu.VMEM)]
+    outs = [pl.BlockSpec(memory_space=pltpu.VMEM)] * 2
     args = [part, resid_sq]
     if resid is not None:
         kept, held, _ = resid.shape
@@ -401,8 +424,8 @@
             real[rows, :] = total[rows, :sources].astype(jnp.float32)
             imag[rows, :] = total[rows, sources:].astype(jnp.float32)
 
-    residual_norm = jnp.sum(norms[0], axis=(0, 1), keepdims=True)
-    direction_norm = jnp.sum(norms[1], axis=(0, 1), keepdims=True)
+    residual_norm = jnp.sum(norms[:4], axis=(0, 1), keepdims=True)
+    direction_norm = jnp.sum(norms[4:], axis=(0, 1), keepdims=True)
     step_size = 0.5 * residual_norm / (direction_norm + 1e-06)
     threshold = shrink[...] * (step_size * jnp.sqrt(direction_norm / count_total))
     threshold = jnp.concatenate([threshold, threshold], axis=1)
@@ -428,13 +451,9 @@
 
 
 def products_kernel(core_ref, near, far, spectra, near_data, far_data, near_res, far_res, part, square):
-    held = near.shape[2]
-    points = spectra.shape[0] * spectra.shape[2]
-    width = spectra.shape[3]
+    batch, _, held, _ = near.shape
+    everywhere, _, each, width = spectra.shape
     sources = width // 2
-    values = spectra[...].reshape(points, width)
-    real_op = jnp.concatenate([near[0, 0], far[0, 0]], axis=0)
-    imag_op = jnp.concatenate([near[0, 1], far[0, 1]], axis=0)
 
     def product(left, right, side):
         return lax.dot_general(
@@ -444,20 +463,25 @@
     def turned(values):
         return jnp.concatenate([-values[:, sources:], values[:, :sources]], axis=1)
 
-    predicted = product(real_op, values, 1) + product(imag_op, turned(values), 1)
-    recorded = jnp.concatenate([near_data[0, 0], far_data[0]], axis=0).astype(jnp.float32)
-    resid = (recorded - predicted).astype(jnp.bfloat16)
-    near_res[0] = resid[:held]
-    far_res[0] = resid[held:]
-
     @pl.when(pl.program_id(0) == 0)
     def clear():
         square[...] = jnp.zeros_like(square)
 
-    wide = resid.astype(jnp.float32)
-    square[...] += jnp.sum((wide * wide).reshape(-1, 8, width), axis=0)
-    direction = product(real_op, resid, 0) - product(imag_op, turned(resid), 0)
-    part[...] = direction.astype(jnp.bfloat16).reshape(part.shape)
+    added = jnp.zeros(square.shape, jnp.float32)
+    for k in range(batch):
+        values = spectra[:, k].reshape(everywhere * each, width)
+        real_op = jnp.concatenate([near[k, 0], far[k, 0]], axis=0)
+        imag_op = jnp.concatenate([near[k, 1], far[k, 1]], axis=0)
+        predicted = product(real_op, values, 1) + product(imag_op, turned(values), 1)
+        recorded = jnp.concatenate([near_data[0, k], far_data[k]], axis=0).astype(jnp.float32)
+        resid = (recorded - predicted).astype(jnp.bfloat16)
+        near_res[k] = resid[:held]
+        far_res[k] = resid[held:]
+        wide = resid.astype(jnp.float32)
+        added += jnp.sum((wide * wide).reshape(-1, 8, width), axis=0)
+        direction = product(real_op, resid, 0) - product(imag_op, turned(resid), 0)
+        part[:, k] = direction.astype(jnp.bfloat16).reshape(everywhere, each, width)
+    square[...] += added
 
 
 def params():
@@ -509,19 +533,20 @@
 def products(core, near, far, spectra, near_data, far_data):
     kept, _, held, _ = far.shape
     everywhere, _, points, width = spectra.shape
-    rows = pl.BlockSpec((1, held, width), lambda k, c: (k, 0, 0))
-    spread_block = pl.BlockSpec((everywhere, 1, points, width), lambda k, c: (0, k, 0, 0))
+    batch = math.gcd(kept, 4)
+    rows = pl.BlockSpec((batch, held, width), lambda k, c: (k, 0, 0))
+    spread_block = pl.BlockSpec((everywhere, batch, points, width), lambda k, c: (0, k, 0, 0))
     resid_shape = jax.ShapeDtypeStruct((kept, held, width), jnp.bfloat16)
     return pl.pallas_call(
         products_kernel,
         grid_spec=pltpu.PrefetchScalarGridSpec(
             num_scalar_prefetch=1,
-            grid=(kept,),
+            grid=(kept // batch,),
             in_specs=[
-                pl.BlockSpec((1,) + far.shape[1:], lambda k, c: (c[0] * kept + k, 0, 0, 0)),
-                pl.BlockSpec((1,) + far.shape[1:], lambda k, c: (k, 0, 0, 0)),
+                pl.BlockSpec((batch,) + far.shape[1:], lambda k, c: (c[0] * (kept // batch) + k, 0, 0, 0)),
+                pl.BlockSpec((batch,) + far.shape[1:], lambda k, c: (k, 0, 0, 0)),
                 spread_block,
-                pl.BlockSpec((1, 1, held, width), lambda k, c: (c[0], k, 0, 0)),
+                pl.BlockSpec((1, batch, held, width), lambda k, c: (c[0], k, 0, 0)),
                 rows,
             ],
             out_specs=[rows, rows, spread_block, pl.BlockSpec((8, width), lambda k, c: (0, 0))],
@@ -549,7 +574,7 @@
 
 def plain_advance(norms, shrink, total, prim, turned_table, table, count_total, last):
     points, samples, sources = prim.shape
-    residual_norm, direction_norm = jnp.sum(norms[0]), jnp.sum(norms[1])
+    residual_norm, direction_norm = jnp.sum(norms[:4]), jnp.sum(norms[4:])
     step_size = 0.5 * residual_norm / (direction_norm + 1e-06)
     threshold = shrink[:, None, :] * (step_size * jnp.sqrt(direction_norm / count_total))
     update = jnp.einsum(

time: 662 us -> 579 us (0.87)
  Pallas kernels: 642 us -> 560 us
    pallas_call x2, Pallas kernels: 283 us -> 236 us  [collect(): pl.pallas_call(functools.partial(collect_kernel, freqs, groups, resid is...]
    pallas_call x2, Pallas kernels: 68.9 us -> 37 us  [products(): pl.pallas_call(products_kernel, grid_spec=pltpu.PrefetchScalarGridSpec(nu...]
where the time goes in v3:
time: 579 us; the launch traced here: 578 us
  Pallas kernels  560 us (97%)
  local copies, waits for them, and re-layouts  17 us (3%)
    pallas_call x2, Pallas kernels, collect(): pl.pallas_call(functools.partial(collect_kernel, freqs, groups, resid is...  236 us
    pallas_call x2, Pallas kernels, spread(): pl.pallas_call(functools.partial(spread_kernel, freqs, groups, operator i...  234 us
    pallas_call x2, Pallas kernels, advance(): pl.pallas_call(functools.partial(update_kernel, count_total, last), grid=...  41.1 us
    pallas_call x2, Pallas kernels, products(): pl.pallas_call(products_kernel, grid_spec=pltpu.PrefetchScalarGridSpec(nu...  37 us
    pallas_call x1, Pallas kernels, forward(): pl.pallas_call(forward_kernel, grid=(points // 2,), out_shape=jax.ShapeDt...  12.8 us

profile of v3, /device:TPU:0, one launch (start us, length us, event | category | flops | bytes accessed | tf_op | source)
XLA Modules:
  0.0 578.0 jit_solution(12263013949759290126)
XLA Ops:
  0.6 4.6 reshape.52
  5.2 3.4 copy.12
  8.7 12.8 %shard_map.77 = bf16[8192,256]{1,0:T(8,128)(2,1)} custom-call(f32[16,1024,128]{2,1,0:T(8,128)} %refs_3_.1, bf16[1024,1024]{1,0:T(8,128)(2,1)} %constant.13.clone.table.refs_5_), custom_call_target="tpu_custom_call" | custom-call | tf_op jit(solution)/shard_map/pallas_call | solution.py:498
  21.5 118.5 %shard_map.78 = (bf16[32,512,256]{2,1,0:T(8,128)(2,1)}, bf16[32,2,96,512]{3,2,1,0:T(8,128)(2,1)}, bf16[32,96,256]{2,1,0:T(8,128)(2,1)}) custom-call(bf16[16,512,256]{2,1,0:T(8,128)(2,1)} %bitcast.20, bf16[64,2,96,512]{3,2,1,0:T(8,128)(2,1)} %near.3, bf16[2,32,96,256]{3,2,1,0:T(8,128)(2,1)} %bitcast.16), custom_call_target="tpu_custom_call" | custom-call | tf_op jit(solution)/shard_map/pallas_call | solution.py:314
  140.0 18.5 %shard_map.79 = (bf16[32,96,256]{2,1,0:T(8,128)(2,1)}, bf16[32,96,256]{2,1,0:T(8,128)(2,1)}, bf16[32,32,16,256]{3,2,1,0:T(8,128)(2,1)}, f32[8,256]{1,0:T(8,128)}) custom-call(s32[1]{0:T(128)} %bitcast.core_ref, bf16[64,2,96,512]{3,2,1,0:T(8,128)(2,1)} %near.3, bf16[32,2,96,512]{3,2,1,0:T(8,128)(2,1)} %get-tuple-element.18.far, ...), custom_call_target="tpu_custom_call" | custom-call | tf_op jit(solution)/shard_map/pallas_call | solution.py:540
  158.5 117.8 %shard_map.80 = (bf16[16,512,256]{2,1,0:T(8,128)(2,1)}, f32[8,128]{1,0:T(8,128)}) custom-call(bf16[32,512,256]{2,1,0:T(8,128)(2,1)} %bitcast.22, f32[8,256]{1,0:T(8,128)} %get-tuple-element.22.refs_1_), custom_call_target="tpu_custom_call" | custom-call | tf_op jit(solution)/shard_map/pallas_call | solution.py:356
  276.3 26.8 %shard_map.81 = (f32[16,1024,128]{2,1,0:T(8,128)}, bf16[8192,256]{1,0:T(8,128)(2,1)}) custom-call(f32[8,128]{1,0:T(8,128)} %get-tuple-element.23.refs_0_, f32[1,128]{1,0:T(1,128)} %bitcast.28, bf16[8192,256]{1,0:T(8,128)(2,1)} %bitcast.26, f32[16,1024,128]{2,1,0:T(8,128)} %refs_3_.1, bf16[1024,1024]{1,0:T(8,128)(2,1)} %constant.14.clone.refs_4_, ...), custom_call_target="tpu_custom_call" | custom-call | tf_op jit(solution)/shard_map/pallas_call | solution.py:522
  303.2 115.4 %shard_map.82 = bf16[32,512,256]{2,1,0:T(8,128)(2,1)} custom-call(bf16[16,512,256]{2,1,0:T(8,128)(2,1)} %bitcast.24), custom_call_target="tpu_custom_call" | custom-call | tf_op jit(solution)/shard_map/pallas_call | solution.py:314
  418.6 18.5 %shard_map.83 = (bf16[32,96,256]{2,1,0:T(8,128)(2,1)}, bf16[32,96,256]{2,1,0:T(8,128)(2,1)}, bf16[32,32,16,256]{3,2,1,0:T(8,128)(2,1)}, f32[8,256]{1,0:T(8,128)}) custom-call(s32[1]{0:T(128)} %bitcast.core_ref, bf16[64,2,96,512]{3,2,1,0:T(8,128)(2,1)} %near.3, bf16[32,2,96,512]{3,2,1,0:T(8,128)(2,1)} %get-tuple-element.18.far, ...), custom_call_target="tpu_custom_call" | custom-call | tf_op jit(solution)/shard_map/pallas_call | solution.py:540
  437.1 117.7 %shard_map.84 = (bf16[16,512,256]{2,1,0:T(8,128)(2,1)}, f32[8,128]{1,0:T(8,128)}, bf16[64,96,256]{2,1,0:T(8,128)(2,1)}) custom-call(bf16[32,512,256]{2,1,0:T(8,128)(2,1)} %bitcast.21, f32[8,256]{1,0:T(8,128)} %get-tuple-element.27.refs_1_, bf16[32,96,256]{2,1,0:T(8,128)(2,1)} %get-tuple-element.28.refs_2_, bf16[32,96,256]{2,1,0:T(8,128)(2,1)} %get-tuple-element.29.refs_3_), custom_call_target="tpu_custom_call" | custom-call | tf_op jit(solution)/shard_map/pallas_call | solution.py:356
  554.7 14.3 %shard_map.85 = f32[16,1024,128]{2,1,0:T(8,128)} custom-call(f32[8,128]{1,0:T(8,128)} %get-tuple-element.30.refs_0_, f32[1,128]{1,0:T(1,128)} %bitcast.29, bf16[8192,256]{1,0:T(8,128)(2,1)} %bitcast.25, f32[16,1024,128]{2,1,0:T(8,128)} %get-tuple-element.32.refs_3_, bf16[1024,1024]{1,0:T(8,128)(2,1)} %constant.14.clone.refs_4_), custom_call_target="tpu_custom_call" | custom-call | tf_op jit(solution)/shard_map/pallas_call | solution.py:522
  569.0 3.8 reshape.51
  572.8 5.2 copy.9

commit v4 on v3

--- a/solution.py
+++ b/solution.py
@@ -12,6 +12,7 @@
 ITERS = 2
 CORES = 2
 SWAPS = 8
+BATCH = 4
 MESH = pl.DeviceIdType.MESH
 VMEM_LIMIT = 56 * 1024 * 1024
 
@@ -311,11 +312,12 @@
         sems += [dma((SWAPS + 1,)), dma((SWAPS + 1,))]
         args += [operator, data]
     anywhere = pl.BlockSpec(memory_space=pl.ANY)
+    held_in = pl.BlockSpec(memory_space=pltpu.VMEM)
     return pl.pallas_call(
         functools.partial(spread_kernel, freqs, groups, operator is not None),
         out_shape=shapes,
-        in_specs=[anywhere] * len(args),
-        out_specs=[anywhere] * len(shapes),
+        in_specs=[held_in] + [anywhere] * (len(args) - 1),
+        out_specs=[held_in] + [anywhere] * (len(shapes) - 1),
         scratch_shapes=sems,
         compiler_params=pltpu.CompilerParams(
             collective_id=ident, has_side_effects=True, vmem_limit_bytes=VMEM_LIMIT
@@ -387,18 +389,22 @@
             )
 
 
-def pair_of(prim):
-    return jnp.concatenate([prim[0], prim[1]], axis=1)
+def pair_of(prim, first):
+    return jnp.concatenate([prim[first], prim[first + 1]], axis=1)
 
 
 def forward_kernel(prim, table, out, *scratch):
     sources = prim.shape[2]
     frequencies = table.shape[0] // 2
     step = pl.program_id(0)
-    value = jnp.dot(
-        table[...], pair_of(prim).astype(jnp.bfloat16), preferred_element_type=jnp.float32
-    )
-    interleave(value, scratch, 2 * step, sources, frequencies)
+    batch = prim.shape[0]
+    for first in range(0, batch, 2):
+        value = jnp.dot(
+            table[...],
+            pair_of(prim, first).astype(jnp.bfloat16),
+            preferred_element_type=jnp.float32,
+        )
+        interleave(value, scratch, batch * step + first, sources, frequencies)
 
     @pl.when(step == pl.num_programs(0) - 1)
     def finish():
@@ -434,16 +440,22 @@
         rows = pl.ds(point, frequencies, stride=stride)
         return jnp.concatenate([real[rows, :], imag[rows, :]], axis=0).astype(jnp.bfloat16)
 
-    both = jnp.concatenate([column(2 * step), column(2 * step + 1)], axis=1)
-    update = jnp.dot(turned_table[...], both, preferred_element_type=jnp.float32)
-    moved = pair_of(prim) + step_size * update
-    fresh = moved - jnp.clip(moved, -threshold, threshold)
-    prim_out[0] = fresh[:, :sources]
-    prim_out[1] = fresh[:, sources:]
+    batch = prim.shape[0]
+    for first in range(0, batch, 2):
+        point = batch * step + first
+        both = jnp.concatenate([column(point), column(point + 1)], axis=1)
+        update = jnp.dot(turned_table[...], both, preferred_element_type=jnp.float32)
+        moved = pair_of(prim, first) + step_size * update
+        fresh = moved - jnp.clip(moved, -threshold, threshold)
+        prim_out[first] = fresh[:, :sources]
+        prim_out[first + 1] = fresh[:, sources:]
+        if not last:
+            value = jnp.dot(
+                table[...], fresh.astype(jnp.bfloat16), preferred_element_type=jnp.float32
+            )
+            interleave(value, scratch, point, sources, frequencies)
     if last:
         return
-    value = jnp.dot(table[...], fresh.astype(jnp.bfloat16), preferred_element_type=jnp.float32)
-    interleave(value, scratch, 2 * step, sources, frequencies)
 
     @pl.when(step == pl.num_programs(0) - 1)
     def finish():
@@ -497,9 +509,9 @@
     rows = table.shape[0] // 2 * points
     return pl.pallas_call(
         forward_kernel,
-        grid=(points // 2,),
+        grid=(points // BATCH,),
         out_shape=jax.ShapeDtypeStruct((rows, 2 * sources), jnp.bfloat16),
-        in_specs=[pl.BlockSpec((2, samples, sources), lambda i: (i, 0, 0)), once(table.shape)],
+        in_specs=[pl.BlockSpec((BATCH, samples, sources), lambda i: (i, 0, 0)), once(table.shape)],
         out_specs=once((rows, 2 * sources)),
         scratch_shapes=[pltpu.VMEM((rows, sources), jnp.float32)] * 2,
         compiler_params=params(),
@@ -509,7 +521,7 @@
 def advance(norms, shrink, total, prim, turned_table, table, count_total, last):
     points, samples, sources = prim.shape
     rows = total.shape[0]
-    block = pl.BlockSpec((2, samples, sources), lambda i: (i, 0, 0))
+    block = pl.BlockSpec((BATCH, samples, sources), lambda i: (i, 0, 0))
     args = [norms, shrink, total, prim, turned_table]
     specs = [once(norms.shape), once(shrink.shape), once(total.shape), block, once(turned_table.shape)]
     shapes, outs = [jax.ShapeDtypeStruct(prim.shape, jnp.float32)], [block]
@@ -521,7 +533,7 @@
         outs.append(once(total.shape))
     return pl.pallas_call(
         functools.partial(update_kernel, count_total, last),
-        grid=(points // 2,),
+        grid=(points // BATCH,),
         out_shape=shapes,
         in_specs=specs,
         out_specs=outs,

time: 579 us -> 582 us (level)
    pallas_call x2, Pallas kernels: 234 us -> 243 us  [spread(): pl.pallas_call(functools.partial(spread_kernel, freqs, groups, operator i...]
where the time goes in v4:
time: 582 us; the launch traced here: 581 us
  Pallas kernels  563 us (97%)
  local copies, waits for them, and re-layouts  17 us (3%)
    pallas_call x2, Pallas kernels, spread(): pl.pallas_call(functools.partial(spread_kernel, freqs, groups, operator i...  243 us
    pallas_call x2, Pallas kernels, collect(): pl.pallas_call(functools.partial(collect_kernel, freqs, groups, resid is...  235 us
    pallas_call x2, Pallas kernels, products(): pl.pallas_call(products_kernel, grid_spec=pltpu.PrefetchScalarGridSpec(nu...  37.2 us
    pallas_call x2, Pallas kernels, advance(): pl.pallas_call(functools.partial(update_kernel, count_total, last), grid=...  35.5 us

profile of v4, /device:TPU:0, one launch (start us, length us, event | category | flops | bytes accessed | tf_op | source)
XLA Modules:
  0.0 580.6 jit_solution(4674477640158468877)
XLA Ops:
  0.6 4.6 reshape.52
  5.2 3.4 copy.12
  8.7 11.5 %shard_map.77 = bf16[8192,256]{1,0:T(8,128)(2,1)} custom-call(f32[16,1024,128]{2,1,0:T(8,128)} %refs_3_.1, bf16[1024,1024]{1,0:T(8,128)(2,1)} %constant.13.clone.table.refs_5_), custom_call_target="tpu_custom_call" | custom-call | tf_op jit(solution)/shard_map/pallas_call | solution.py:510
  20.1 123.3 %shard_map.78 = (bf16[32,512,256]{2,1,0:T(8,128)(2,1)}, bf16[32,2,96,512]{3,2,1,0:T(8,128)(2,1)}, bf16[32,96,256]{2,1,0:T(8,128)(2,1)}) custom-call(bf16[16,512,256]{2,1,0:T(8,128)(2,1)} %bitcast.20, bf16[64,2,96,512]{3,2,1,0:T(8,128)(2,1)} %near.3, bf16[2,32,96,256]{3,2,1,0:T(8,128)(2,1)} %bitcast.16), custom_call_target="tpu_custom_call" | custom-call | tf_op jit(solution)/shard_map/pallas_call | solution.py:316
  143.4 18.5 %shard_map.79 = (bf16[32,96,256]{2,1,0:T(8,128)(2,1)}, bf16[32,96,256]{2,1,0:T(8,128)(2,1)}, bf16[32,32,16,256]{3,2,1,0:T(8,128)(2,1)}, f32[8,256]{1,0:T(8,128)}) custom-call(s32[1]{0:T(128)} %bitcast.core_ref, bf16[64,2,96,512]{3,2,1,0:T(8,128)(2,1)} %near.3, bf16[32,2,96,512]{3,2,1,0:T(8,128)(2,1)} %get-tuple-element.18.far, ...), custom_call_target="tpu_custom_call" | custom-call | tf_op jit(solution)/shard_map/pallas_call | solution.py:552
  161.9 117.8 %shard_map.80 = (bf16[16,512,256]{2,1,0:T(8,128)(2,1)}, f32[8,128]{1,0:T(8,128)}) custom-call(bf16[32,512,256]{2,1,0:T(8,128)(2,1)} %bitcast.22, f32[8,256]{1,0:T(8,128)} %get-tuple-element.22.refs_1_), custom_call_target="tpu_custom_call" | custom-call | tf_op jit(solution)/shard_map/pallas_call | solution.py:358
  279.8 23.0 %shard_map.81 = (f32[16,1024,128]{2,1,0:T(8,128)}, bf16[8192,256]{1,0:T(8,128)(2,1)}) custom-call(f32[8,128]{1,0:T(8,128)} %get-tuple-element.23.refs_0_, f32[1,128]{1,0:T(1,128)} %bitcast.28, bf16[8192,256]{1,0:T(8,128)(2,1)} %bitcast.26, f32[16,1024,128]{2,1,0:T(8,128)} %refs_3_.1, bf16[1024,1024]{1,0:T(8,128)(2,1)} %constant.14.clone.refs_4_, ...), custom_call_target="tpu_custom_call" | custom-call | tf_op jit(solution)/shard_map/pallas_call | solution.py:534
  302.7 120.1 %shard_map.82 = bf16[32,512,256]{2,1,0:T(8,128)(2,1)} custom-call(bf16[16,512,256]{2,1,0:T(8,128)(2,1)} %bitcast.24), custom_call_target="tpu_custom_call" | custom-call | tf_op jit(solution)/shard_map/pallas_call | solution.py:316
  422.9 18.7 %shard_map.83 = (bf16[32,96,256]{2,1,0:T(8,128)(2,1)}, bf16[32,96,256]{2,1,0:T(8,128)(2,1)}, bf16[32,32,16,256]{3,2,1,0:T(8,128)(2,1)}, f32[8,256]{1,0:T(8,128)}) custom-call(s32[1]{0:T(128)} %bitcast.core_ref, bf16[64,2,96,512]{3,2,1,0:T(8,128)(2,1)} %near.3, bf16[32,2,96,512]{3,2,1,0:T(8,128)(2,1)} %get-tuple-element.18.far, ...), custom_call_target="tpu_custom_call" | custom-call | tf_op jit(solution)/shard_map/pallas_call | solution.py:552
  441.5 117.6 %shard_map.84 = (bf16[16,512,256]{2,1,0:T(8,128)(2,1)}, f32[8,128]{1,0:T(8,128)}, bf16[64,96,256]{2,1,0:T(8,128)(2,1)}) custom-call(bf16[32,512,256]{2,1,0:T(8,128)(2,1)} %bitcast.21, f32[8,256]{1,0:T(8,128)} %get-tuple-element.27.refs_1_, bf16[32,96,256]{2,1,0:T(8,128)(2,1)} %get-tuple-element.28.refs_2_, bf16[32,96,256]{2,1,0:T(8,128)(2,1)} %get-tuple-element.29.refs_3_), custom_call_target="tpu_custom_call" | custom-call | tf_op jit(solution)/shard_map/pallas_call | solution.py:358
  559.2 12.5 %shard_map.85 = f32[16,1024,128]{2,1,0:T(8,128)} custom-call(f32[8,128]{1,0:T(8,128)} %get-tuple-element.30.refs_0_, f32[1,128]{1,0:T(1,128)} %bitcast.29, bf16[8192,256]{1,0:T(8,128)(2,1)} %bitcast.25, f32[16,1024,128]{2,1,0:T(8,128)} %get-tuple-element.32.refs_3_, bf16[1024,1024]{1,0:T(8,128)(2,1)} %constant.14.clone.refs_4_), custom_call_target="tpu_custom_call" | custom-call | tf_op jit(solution)/shard_map/pallas_call | solution.py:534
  571.7 3.8 reshape.51
  575.4 5.2 copy.9
